TPU v7x, 256 devices: a whole 4x4x8 slice. The times are simulated.
256 devices in a mesh: dom: 64 (over y, z, core), rep: 4 (over x).
Axes of the slice: x: 4, y: 4, z: 8, core: 2. Of those that a mesh axis runs over, the one named last changes fastest.
Arguments:
- embeddings: bfloat16 [98304, 1024], P(('dom', 'rep')), may hold values from -6 to 6
- endpoint_pairs: int32 [32768, 2], P(('dom', 'rep')), may hold values from 0 to 98303, as said below
- node_slot: int32 [98304], replicated, may hold values from 0 to 98303, as said below
- first_weight: bfloat16 [2048, 1024], replicated, may hold values from -0.125 to 0.125
- second_weight: bfloat16 [1024, 1024], replicated, may hold values from -0.1875 to 0.1875
- score_weight: bfloat16 [1024], replicated, may hold values from -0.1875 to 0.1875
- score_grad: float32 [32768], P(('dom', 'rep')), may hold values from -48 to 48
Outputs:
- link_score: float32 [32768], P(('dom', 'rep'))
- node_grad: float32 [98304, 1024], P(('dom', 'rep'))
- first_grad: float32 [2048, 1024], P(('dom', 'rep'))
- second_grad: float32 [1024, 1024], P(('dom', 'rep'))
- head_grad: float32 [1024], replicated
Inputs may be any that keep to these rules, and one draw needn't show every extreme that they name: node_slot is a permutation of the table positions; position s is held by the device of index s // 384 over dom+rep. `endpoint_pairs`: among the endpoints of one side of the pairs of one device, at most 2 have positions held by any one device, and in every such group some device holds exactly 2.
All inputs are finite; a program needn't handle non-finite values.
Results may differ from a plain program's by a relative error of at most 0.005.
Values may be sent and summed in bfloat16 or wider, within the bound.
A program may use at most 128 MiB of HBM per device.

v0:
```python
import jax
import jax.numpy as jnp
from jax import lax
from jax.sharding import PartitionSpec as P


def gelu_slope(values):
    return jax.jvp(jax.nn.gelu, (values,), (jnp.ones_like(values),))


def shards(
    embeddings, endpoint_pairs, node_slot, first_weight, second_weight, score_weight, score_grad
):
    dom_count = lax.axis_size("dom")
    rep_count = lax.axis_size("rep")
    dev_count = dom_count * rep_count
    node_rows, width = embeddings.shape
    edge_count = endpoint_pairs.shape[0]
    capacity = max(2, (2 * edge_count + dev_count - 1) // dev_count)
    slot_total = dev_count * 2 * capacity
    slots = node_slot[endpoint_pairs]
    owner = slots // node_rows
    local_row = slots % node_rows
    device_ids = jnp.arange(dev_count, dtype=jnp.int32)
    owner_hits = (owner[:, :, None] == device_ids[None, None, :]).astype(jnp.int32)
    slot_rank = jnp.sum(jnp.cumsum(owner_hits, axis=0) * owner_hits, axis=2) - 1
    side_index = jnp.arange(2, dtype=jnp.int32)[None, :]
    position = (owner * (2 * capacity) + side_index * capacity + slot_rank).reshape(-1)
    requests = jnp.zeros((slot_total,), jnp.int32).at[position].set(local_row.reshape(-1))
    requests = requests.reshape(dom_count, rep_count, 2, capacity)
    asked = lax.all_to_all(
        lax.all_to_all(requests, "dom", split_axis=0, concat_axis=0, tiled=True),
        "rep",
        split_axis=1,
        concat_axis=1,
        tiled=True,
    )
    found = embeddings[asked]
    arrived = lax.all_to_all(
        lax.all_to_all(found, "dom", split_axis=0, concat_axis=0, tiled=True),
        "rep",
        split_axis=1,
        concat_axis=1,
        tiled=True,
    )
    arrived_rows = arrived.reshape(slot_total, width)
    features = arrived_rows[position].reshape(edge_count, 2 * width)
    first_pre = jnp.dot(features, first_weight, preferred_element_type=jnp.float32)
    first_val, first_slope = gelu_slope(first_pre)
    first_act = first_val.astype(jnp.bfloat16)
    second_pre = jnp.dot(first_act, second_weight, preferred_element_type=jnp.float32)
    second_val, second_slope = gelu_slope(second_pre)
    second_act = second_val.astype(jnp.bfloat16)
    link_score = jnp.dot(second_act, score_weight, preferred_element_type=jnp.float32)
    head_local = jnp.dot(
        score_grad, second_act.astype(jnp.float32), precision=lax.Precision.HIGHEST
    )
    head_grad = lax.psum(head_local, ("dom", "rep"))
    second_delta = (
        score_grad[:, None] * score_weight.astype(jnp.float32)[None, :] * second_slope
    ).astype(jnp.bfloat16)
    back_second = lax.dot_general(
        second_delta, second_weight, (((1,), (1,)), ((), ())), preferred_element_type=jnp.float32
    )
    first_delta = (back_second * first_slope).astype(jnp.bfloat16)
    columns = first_act
    second_grad = lax.psum_scatter(
        lax.dot_general(
            columns, second_delta, (((0,), (0,)), ((), ())), preferred_element_type=jnp.float32
        ),
        ("dom", "rep"),
        scatter_dimension=0,
        tiled=True,
    )
    columns = features
    first_grad = lax.psum_scatter(
        lax.dot_general(
            columns, first_delta, (((0,), (0,)), ((), ())), preferred_element_type=jnp.float32
        ),
        ("dom", "rep"),
        scatter_dimension=0,
        tiled=True,
    )
    feature_grad = lax.dot_general(
        first_delta, first_weight, (((1,), (1,)), ((), ())), preferred_element_type=jnp.float32
    )
    outgoing = (
        jnp.zeros((slot_total, width), jnp.float32)
        .at[position]
        .set(feature_grad.reshape(edge_count * 2, width))
    )
    outgoing = outgoing.reshape(dom_count, rep_count, 2, capacity, width)
    returned = lax.all_to_all(
        lax.all_to_all(outgoing, "dom", split_axis=0, concat_axis=0, tiled=True),
        "rep",
        split_axis=1,
        concat_axis=1,
        tiled=True,
    )
    contrib = returned.reshape(slot_total, width)
    node_grad = jnp.zeros((node_rows, width), jnp.float32).at[asked.reshape(-1)].add(contrib)
    return (link_score, node_grad, first_grad, second_grad, head_grad)


def solution(mesh):
    in_specs = (
        P(("dom", "rep"), None),
        P(("dom", "rep"), None),
        P(),
        P(),
        P(),
        P(),
        P(("dom", "rep")),
    )
    out_specs = (
        P(("dom", "rep")),
        P(("dom", "rep"), None),
        P(("dom", "rep"), None),
        P(("dom", "rep"), None),
        P(),
    )
    return jax.shard_map(shards, mesh=mesh, in_specs=in_specs, out_specs=out_specs, check_vma=False)
```

profile of v0, /device:TPU:1, one launch (start us, length us, event | category | flops | bytes accessed | tf_op | source)
XLA Modules:
  0.0 1753.3 jit_solution(11727255916684776976)
XLA Ops:
  7.2 0.8 compare_select_fusion.3
  8.3 2.2 gather_fusion
  10.9 2.6 select_reduce_fusion
  13.8 1.4 scatter_custom_fusion
  15.2 0.4 reshape.174
  15.6 0.9 copy.30
  16.5 23.3 %all_to_all.30 = s32[64,4,2,2]{1,3,2,0:T(2,128)S(1)} all-to-all(s32[64,4,2,2]{1,3,2,0:T(2,128)S(1)} %copy.30), channel_id=1, replica_groups=mesh['dom'=64,'rep'=4] {'dom'}, dimensions={0} | all-to-all | bytes 8192 | tf_op jit(solution)/shard_map/all_to_all | solution.py:32
  40.0 8.0 all_to_all.31
  48.0 0.5 broadcast.250
  48.5 0.7 reduce
  49.2 0.2 copy.32
  49.5 0.3 reshape.191
  49.8 5.4 gather_fusion.1
  55.2 4.1 reshape.190
  59.3 57.6 %all_to_all.32 = bf16[64,4,2,2,1024]{4,3,2,1,0:T(2,128)(2,1)S(1)} all-to-all(bf16[64,4,2,2,1024]{4,3,2,1,0:T(2,128)(2,1)} %reshape.190), channel_id=1, replica_groups=mesh['dom'=64,'rep'=4] {'dom'}, dimensions={0} | all-to-all | bytes 4194304 | tf_op jit(solution)/shard_map/all_to_all | solution.py:40
  116.8 2.9 copy.33
  119.8 4.4 all-to-all-start.3
  124.2 0.2 all-reduce.3.cloned.1.call-start
  124.5 25.8 %all-to-all-done.3 = bf16[64,4,2,2,1024]{4,3,2,0,1:T(2,128)(2,1)} async-done(((bf16[64,4,2,2,1024]{4,3,2,0,1:T(2,128)(2,1)}), bf16[64,4,2,2,1024]{4,3,2,0,1:T(2,128)(2,1)}, u32[]{:S(2)}, u32[]{:S(2)}) %all-to-all-start.3) | async-done | bytes 2097184 | tf_op jit(solution)/shard_map/all_to_all | solution.py:39
  150.3 5.4 copy.34
  155.7 4.1 reshape.175
  159.8 3.4 gather_fusion.2
  163.2 0.2 reshape.176
  163.4 2.9 fusion.40
  166.3 0.6 multiply_convert_fusion
  167.0 0.8 copy-done.3
  167.8 3.1 fusion.36
  170.9 2.1 fusion.2
  173.0 0.7 copy-done.2
  173.7 4.5 fusion.42
  178.2 3.8 fusion.41
  182.0 1.1 reshape.217
  183.2 4.2 scatter_custom_fusion.1
  187.4 5.8 reshape.179
  193.3 108.5 %all_to_all.33 = f32[64,4,2,2,1024]{4,3,2,1,0:T(2,128)S(1)} all-to-all(f32[64,4,2,2,1024]{4,3,2,1,0:T(2,128)} %reshape.179), channel_id=1, replica_groups=mesh['dom'=64,'rep'=4] {'dom'}, dimensions={0} | all-to-all | bytes 8388608 | tf_op jit(solution)/shard_map/all_to_all | solution.py:94
  301.8 3.9 copy.36
  305.7 4.9 all-to-all-start.5
  310.6 0.2 copy.35
  310.8 0.3 reshape.177
  311.1 0.2 fusion.34
  311.4 113.4 %psum.7 = f32[1024]{0:T(1024)} all-reduce(f32[1024]{0:T(1024)S(1)} %bitcast.25), channel_id=1, replica_groups=mesh['dom'=64,'rep'=4] {'dom','rep'}, use_global_device_ids=true, to_apply=%region_7.8 | all-reduce | flops 1024 | bytes 8192 | tf_op jit(solution)/shard_map/psum | solution.py:58
  424.7 0.7 convolution_bitcast_fusion
  425.4 44.8 %all-reduce.3.cloned.1.call-done = f32[1024,1024]{1,0:T(8,128)} async-done(((f32[1024,1024]{1,0:T(8,128)}), f32[1024,1024]{1,0:T(8,128)}) %all-reduce.3.cloned.1.call-update) | async-done | bytes 4194320
  470.2 1.4 constant_dynamic-slice_fusion
  471.6 6.9 copy.37
  478.5 6.1 reshape.225
  484.6 11.5 scatter_custom_fusion.2
  496.1 1250.4 %reduce-scatter.2.cloned.1.call-done = f32[8,1024]{1,0:T(8,128)} async-done(((f32[2048,1024]{1,0:T(8,128)}), f32[8,1024]{1,0:T(8,128)}) %reduce-scatter.2.cloned.1.call-update) | async-done | bytes 32784 | tf_op jit(solution)/shard_map/reduce_scatter | solution.py:76
  (37 shorter events, 1.3 us)
Async XLA Ops:
  7.2 159.2 %copy-start = (bf16[1024,1024]{1,0:T(8,128)(2,1)S(1)}, bf16[1024,1024]{1,0:T(8,128)(2,1)}, u32[]{:S(2)}) copy-start(bf16[1024,1024]{1,0:T(8,128)(2,1)} %param.11) | copy-start | bytes 6291460
  10.5 39.3 %copy-start.1 = (bf16[384,1024]{1,0:T(8,128)(2,1)S(1)}, bf16[384,1024]{1,0:T(8,128)(2,1)}, u32[]{:S(2)}) copy-start(bf16[384,1024]{1,0:T(8,128)(2,1)} %param.7) | copy-start | bytes 2359300
  116.8 7.6 copy-start.4
  119.8 30.6 %all-to-all-start.3 = ((bf16[64,4,2,2,1024]{4,3,2,0,1:T(2,128)(2,1)}), bf16[64,4,2,2,1024]{4,3,2,0,1:T(2,128)(2,1)}, u32[]{:S(2)}, u32[]{:S(2)}) async-start(bf16[64,4,2,2,1024]{4,3,2,0,1:T(2,128)(2,1)} %copy.33), calls=%async_computation.3 | async-start | bytes 4194304 | tf_op jit(solution)/shard_map/all_to_all | solution.py:39
  124.2 346.0 %all-reduce.3.cloned.1.call-start = ((), (), s32[]{:S(2)}) async-start(), calls=%async_computation.8 | async-start | bytes 8388608
  163.4 4.4 copy-start.5
  167.0 0.8 copy-start.3
  170.8 1575.7 %reduce-scatter.2.cloned.1.call-start = ((), (), s32[]{:S(2)}) async-start(), calls=%async_computation.7 | async-start | bytes 8421376 | tf_op jit(solution)/shard_map/reduce_scatter | solution.py:76
  173.0 0.7 copy-start.2
  305.7 165.9 %all-to-all-start.5 = ((f32[64,4,2,2,1024]{4,3,2,0,1:T(2,128)}), f32[64,4,2,2,1024]{4,3,2,0,1:T(2,128)}, u32[]{:S(2)}, u32[]{:S(2)}) async-start(f32[64,4,2,2,1024]{4,3,2,0,1:T(2,128)} %copy.36), calls=%async_computation.5 | async-start | bytes 8388608 | tf_op jit(solution)/shard_map/all_to_all | solution.py:93
Sparse Core Ops, SparseCore 0:
  171.0 299.2 all-reduce.2
  473.4 1273.0 reduce-scatter.1
where the time goes:
time: 1760 us; the launch traced here: 1750 us
  waiting for transfers between devices  1320 us (75%)
  blocking collectives  311 us (18%)
  local copies, waits for them, and re-layouts  64.1 us (4%)
  matrix products  17.9 us (1%)
    reduce_scatter x1, waiting for transfers between devices, shards(): lax.psum_scatter(lax.dot_general(columns, first_delta, (((0,), (0,)), (()...  1250 us
    psum x1, blocking collectives, shards(): head_grad = lax.psum(head_local, ('dom', 'rep'))  113 us
    all_to_all x1, blocking collectives, shards(): lax.all_to_all(outgoing, 'dom', split_axis=0, concat_axis=0, tiled=True)  109 us
    all_to_all x1, blocking collectives, shards(): lax.all_to_all(found, 'dom', split_axis=0, concat_axis=0, tiled=True)  57.6 us
    unnamed x3, waiting for transfers between devices  44.8 us
  transfers between devices with their start and end apart: 4, of which 3 were waited for; matrix products, arithmetic and copies ran while one was open for 3% of the time, Pallas kernels for 0%

commit v1 on v0

v1 whole, which is shorter than its diff:
```python
import functools

import jax
import jax.numpy as jnp
from jax import lax
from jax.experimental import pallas as pl
from jax.experimental.pallas import tpu as pltpu
from jax.sharding import PartitionSpec as P

MESH = pl.DeviceIdType.MESH
NY, NZ, NC, NX = 4, 8, 2, 4
NZC, NXY = NZ * NC, NX * NY
NDEV = NZC * NXY
ROWS, WIDTH, HID, EDGES = 384, 1024, 1024, 128
BF, F32 = jnp.bfloat16, jnp.float32
GELU_A, GELU_B = 0.7978845608028654, 0.044715


def dot(a, b):
    return jnp.dot(a, b, preferred_element_type=F32)


def dot_nt(a, b):
    return lax.dot_general(a, b, (((1,), (1,)), ((), ())), preferred_element_type=F32)


def dot_tn(a, b):
    return lax.dot_general(a, b, (((0,), (0,)), ((), ())), preferred_element_type=F32)


def gelu_both(v):
    t = jnp.tanh(GELU_A * (v + GELU_B * (v * v * v)))
    half = 0.5 * (1.0 + t)
    slope = half + 0.5 * v * (1.0 - t * t) * (GELU_A * (1.0 + (3.0 * GELU_B) * (v * v)))
    return v * half, slope


def iota(shape, dim):
    return lax.broadcasted_iota(jnp.int32, shape, dim)


def body(
    code_row, code_col, sgrad_col, sw_row, emb_hbm, w1_hbm, w2_hbm,
    score_out, node_out, first_out, second_out, head_out,
    emb, w1, w2, idx, hot, stage, send_g, recv_g, send_r, recv_r,
    feats, first_act, first_slope, second_act, ft_own, ft, at_own, at, d1, d2, fg,
    pa, pb, ra, rb, sa, sb, r2a, r2b, ta, tb, r3a, r3b, hbuf,
    small, load_sem, ss, rs,
):
    dom = lax.axis_index("dom")
    x = lax.axis_index("rep")
    y, z, c = dom // 16, (dom // 2) % 8, dom % 2
    zc = z * 2 + c
    xy = y * 4 + x
    me = xy * 16 + zc

    def ident(yy, zz, cc, xx):
        return ((yy * 8 + zz) * 2 + cc, xx)

    def zc_peer(k):
        return ident(y, (z + k % 8) % 8, (c + k // 8) % 2, x)

    def xy_peer(k):
        return ident((y + k // 4) % 4, z, c, (x + k % 4) % 4)

    def rcopy(src, dst, sem, dev):
        return pltpu.make_async_remote_copy(
            src_ref=src, dst_ref=dst, send_sem=ss.at[sem], recv_sem=rs.at[sem],
            device_id=dev, device_id_type=MESH,
        )

    def wait_send(ref, sem):
        pltpu.make_async_copy(ref, ref, ss.at[sem]).wait()

    def wait_recv(ref, sem):
        pltpu.make_async_copy(ref, ref, rs.at[sem]).wait()

    loads = [
        pltpu.make_async_copy(emb_hbm, emb, load_sem.at[0]),
        pltpu.make_async_copy(w1_hbm, w1, load_sem.at[1]),
        pltpu.make_async_copy(w2_hbm, w2, load_sem.at[2]),
    ]
    for load in loads:
        load.start()
    idx[pl.ds(me, 1), :] = code_row[...]
    bar = pltpu.get_barrier_semaphore()

    @pl.loop(1, 16)
    def _(k):
        pl.semaphore_signal(bar, inc=1, device_id=zc_peer(k), device_id_type=MESH)
        pl.semaphore_signal(bar, inc=1, device_id=xy_peer(k), device_id_type=MESH)

    pl.semaphore_wait(bar, 30)

    @pl.loop(1, 16)
    def _(k):
        row = idx.at[pl.ds(me, 1)]
        rcopy(row, row, 0, zc_peer(k)).start()

    wait_recv(small, 0)

    @pl.loop(1, 16)
    def _(k):
        rows = idx.at[pl.ds(xy * 16, 16)]
        rcopy(rows, rows, 1, xy_peer(k)).start()

    wait_recv(idx.at[pl.ds(0, 240)], 1)
    wait_send(small, 0)
    wait_send(idx.at[pl.ds(0, 240)], 1)

    before = (iota((128, 128), 0) < iota((128, 128), 1)).astype(BF)
    loads[0].wait()
    for side in range(2):
        codes = idx[:, side * 128:(side + 1) * 128]
        mine = (codes >> 9) == me
        rank = dot(mine.astype(BF), before)
        local = ((codes & 511) + 1).astype(F32)
        for k in range(2):
            s = side * 2 + k
            hit = mine & (rank == float(k))
            want = jnp.sum(jnp.where(hit, local, 0.0), axis=1, keepdims=True).astype(jnp.int32) - 1
            hot[s] = (want == iota((NDEV, ROWS), 1)).astype(BF)

    def spread(s, n, part):
        for h in range(2):
            stage[h, pl.ds(s * 4 + n, NDEV, stride=16), :] = part[:, h * 128:(h + 1) * 128]

    def pack(dst):
        @pl.loop(0, 16)
        def _(i):
            rows = pl.ds(i * 256, 256)
            both = jnp.concatenate([stage[0, rows, :], stage[1, rows, :]], axis=1)
            dst[pl.ds(i * 16, 16)] = both.astype(BF).reshape(16, 16, 256)

    def unpack(src):
        @pl.loop(0, 16)
        def _(i):
            rows = pl.ds(i * 256, 256)
            both = src[pl.ds(i * 16, 16)].reshape(256, 256).astype(F32)
            stage[0, rows, :] = both[:, :128]
            stage[1, rows, :] = both[:, 128:]

    def collect(s, n):
        rows = pl.ds(s * 4 + n, NDEV, stride=16)
        return jnp.concatenate([stage[0, rows, :], stage[1, rows, :]], axis=1).astype(BF)

    def exchange(src, dst, sem, keep_sem):
        own = pltpu.make_async_copy(src.at[me], dst.at[me], load_sem.at[keep_sem])
        own.start()

        @pl.loop(1, NDEV)
        def _(k):
            yy = (y + (k // 32) % 4) % 4
            xx = (x + (k // 8) % 4) % 4
            zz = (z + k % 8) % 8
            cc = (c + k // 128) % 2
            to = (yy * 4 + xx) * 16 + zz * 2 + cc
            rcopy(src.at[to], dst.at[me], sem, ident(yy, zz, cc, xx)).start()

        return own

    for s in range(4):
        for n in range(4):
            spread(s, n, dot(hot[s], emb[:, n * 256:(n + 1) * 256]))
    pack(send_g)
    own_g = exchange(send_g, recv_g, 2, 3)

    earlier = iota((128, 128), 1) < iota((128, 128), 0)
    picks = []
    for side in range(2):
        row_owner = code_row[:, side * 128:(side + 1) * 128] >> 9
        col_owner = code_col[:, side:side + 1] >> 9
        rank = jnp.sum(jnp.where((col_owner == row_owner) & earlier, 1.0, 0.0), axis=1, keepdims=True)
        home = col_owner == iota((128, NDEV), 1)
        for k in range(2):
            picks.append((home & (rank == float(k))).astype(BF))
    loads[1].wait()
    loads[2].wait()

    own_g.wait()
    wait_recv(recv_g.at[pl.ds(0, 255)], 2)
    unpack(recv_g)
    other = ident(y, z, 1 - c, x)
    for side in range(2):
        for n in range(4):
            col = side * 1024 + n * 256
            part = dot(picks[side * 2], collect(side * 2, n)) + dot(picks[side * 2 + 1], collect(side * 2 + 1, n))
            part = part.astype(BF)
            feats[:, col:col + 256] = part
            ft_own[(col // 64):(col // 64) + 4] = part.T.reshape(4, 2, 32, 128)
    rcopy(ft_own.at[:, 1 - c], ft.at[:, :, pl.ds(128, 128)], 3, other).start()
    ft[:, :, 0:128] = ft_own[:, c]

    for n in range(4):
        cols = slice(n * 256, (n + 1) * 256)
        act, slope = gelu_both(dot(feats[...], w1[:, cols]))
        act = act.astype(BF)
        first_act[:, cols] = act
        first_slope[:, cols] = slope
        at_own[n * 8:(n + 1) * 8] = act.T.reshape(8, 2, 16, 128)
    rcopy(at_own.at[:, 1 - c], at.at[:, :, pl.ds(128, 128)], 4, other).start()
    at[:, :, 0:128] = at_own[:, c]

    score = jnp.zeros((1, 128), F32)
    sgrad = sgrad_col[...]
    for n in range(4):
        cols = slice(n * 256, (n + 1) * 256)
        act, slope = gelu_both(dot(first_act[...], w2[:, cols]))
        act = act.astype(BF)
        sw = sw_row[:, cols]
        score += dot_nt(jnp.broadcast_to(sw, (8, 256)), act)[0:1]
        hbuf[0, :, cols] = jnp.sum(sgrad * act.astype(F32), axis=0, keepdims=True)
        d2[0:128, cols] = (sgrad * sw.astype(F32) * slope).astype(BF)
    score_out[...] = score
    rcopy(d2.at[pl.ds(0, 128)], d2.at[pl.ds(128, 128)], 5, other).start()
    rcopy(hbuf.at[0], hbuf.at[1], 6, other).start()

    for n in range(4):
        cols = slice(n * 256, (n + 1) * 256)
        back = dot_nt(d2[0:128, :], w2[cols, :])
        d1[0:128, cols] = (back * first_slope[:, cols]).astype(BF)
    rcopy(d1.at[pl.ds(0, 128)], d1.at[pl.ds(128, 128)], 7, other).start()

    for n in range(8):
        fg[:, n * 256:(n + 1) * 256] = dot_nt(d1[0:128, :], w1[n * 256:(n + 1) * 256, :]).astype(BF)
    for s in range(4):
        for n in range(4):
            col = (s // 2) * 1024 + n * 256
            spread(s, n, dot_tn(picks[s], fg[:, col:col + 256]))
    pack(send_r)

    wait_recv(at.at[:, :, pl.ds(0, 128)], 4)
    wait_recv(d2.at[pl.ds(0, 128)], 5)
    low = iota((8, 8, 512), 1) < 4
    for yy in range(4):
        res = dot(at[yy * 8:(yy + 1) * 8].reshape(128, 256), d2[...]).reshape(8, 16, 1024)
        for pair in range(2):
            lo = res[:, pair * 8:(pair + 1) * 8, :512]
            hi = res[:, pair * 8:(pair + 1) * 8, 512:]
            even = jnp.where(low, lo, pltpu.roll(hi, 4, axis=1))
            odd = jnp.where(low, pltpu.roll(lo, 4, axis=1), hi)
            for bit, part in ((0, even), (1, odd)):
                full = jnp.concatenate([part[:, :, :256], part[:, :, 256:]], axis=1)
                pb[yy, pair * 2 + bit, :, :, 128:384] = full.astype(BF)
    wait_recv(ft.at[:, :, pl.ds(0, 128)], 3)
    wait_recv(d1.at[pl.ds(0, 128)], 7)
    for yy in range(4):
        lhs = ft[yy * 8:(yy + 1) * 8].reshape(256, 256)
        for n in range(2):
            lo = dot(lhs, d1[:, n * 256:(n + 1) * 256]).reshape(8, 4, 8, 256)
            hi = dot(lhs, d1[:, 512 + n * 256:512 + (n + 1) * 256]).reshape(8, 4, 8, 256)
            for xx in range(4):
                full = jnp.concatenate([lo[:, xx], hi[:, xx]], axis=1).astype(BF)
                if n == 0:
                    pa[xx, yy, :, :, 0:256] = full
                else:
                    pa[xx, yy, :, :, 256:384] = full[:, :, :128]
                    pb[yy, xx, :, :, 0:128] = full[:, :, 128:]

    def along(axis, k):
        if axis == "x":
            return ident(y, z, c, (x + k) % 4), (x + k) % 4
        if axis == "y":
            return ident((y + k) % 4, z, c, x), (y + k) % 4
        return ident(y, (z + k) % 8, c, x), (z + k) % 8

    for k in range(1, 4):
        dev, at_x = along("x", k)
        rcopy(pa.at[at_x], ra.at[k - 1], 8, dev).start()
        dev, at_y = along("y", k)
        rcopy(pb.at[at_y], rb.at[k - 1], 9, dev).start()

    own_r = exchange(send_r, recv_r, 10, 4)

    def head_step(base, count, axis, mine, sem):
        for k in range(1, count):
            dev, _ = along(axis, k)
            rcopy(hbuf.at[base + mine], hbuf.at[base + mine], sem, dev).start()

    wait_recv(hbuf.at[0], 6)
    wait_send(hbuf.at[0], 6)
    hbuf[2 + x] = hbuf[0] + hbuf[1]
    head_step(2, 4, "x", x, 11)

    def add4(own, got, out, sec):
        total = own[sec].astype(F32) + got[0, sec].astype(F32) + got[1, sec].astype(F32) + got[2, sec].astype(F32)
        out[sec] = total.astype(BF)

    wait_recv(ra, 8)

    @pl.loop(0, 4)
    def _(i):
        add4(pa.at[x], ra, sa, i)

    for k in range(1, 4):
        dev, at_y = along("y", k)
        rcopy(sa.at[at_y], r2a.at[k - 1], 12, dev).start()
    wait_recv(rb, 9)

    @pl.loop(0, 4)
    def _(i):
        add4(pb.at[y], rb, sb, i)

    for k in range(1, 4):
        dev, at_x = along("x", k)
        rcopy(sb.at[at_x], r2b.at[k - 1], 13, dev).start()

    wait_recv(hbuf.at[pl.ds(2, 3)], 11)
    wait_send(hbuf.at[pl.ds(2, 3)], 11)
    hbuf[6 + y] = hbuf[2] + hbuf[3] + hbuf[4] + hbuf[5]
    head_step(6, 4, "y", y, 14)

    wait_recv(r2a, 12)
    total = sa[y].astype(F32) + r2a[0].astype(F32) + r2a[1].astype(F32) + r2a[2].astype(F32)
    ta[...] = total.astype(BF)
    for k in range(1, 8):
        dev, at_z = along("z", k)
        rcopy(ta.at[at_z], r3a.at[k - 1], 15, dev).start()
    wait_recv(r2b, 13)
    total = sb[x].astype(F32) + r2b[0].astype(F32) + r2b[1].astype(F32) + r2b[2].astype(F32)
    tb[...] = total.astype(BF)
    for k in range(1, 8):
        dev, at_z = along("z", k)
        rcopy(tb.at[at_z], r3b.at[k - 1], 16, dev).start()

    wait_recv(hbuf.at[pl.ds(6, 3)], 14)
    wait_send(hbuf.at[pl.ds(6, 3)], 14)
    hbuf[10 + z] = hbuf[6] + hbuf[7] + hbuf[8] + hbuf[9]
    head_step(10, 8, "z", z, 17)

    wait_recv(r3a, 15)
    wait_recv(r3b, 16)
    left = ta[z].astype(F32)
    right = tb[z].astype(F32)
    for k in range(7):
        left += r3a[k].astype(F32)
        right += r3b[k].astype(F32)
    whole = jnp.concatenate([left, right], axis=1)
    first_out[:, 0:512] = whole[0:8, 0:512]
    first_out[:, 512:1024] = whole[8:16, 0:512]
    second_out[:, 0:256] = whole[0:4, 512:768]
    second_out[:, 512:768] = whole[4:8, 512:768]
    second_out[:, 256:512] = whole[8:12, 512:768]
    second_out[:, 768:1024] = whole[12:16, 512:768]

    wait_recv(hbuf.at[pl.ds(10, 7)], 17)
    head = hbuf[10]
    for k in range(1, 8):
        head += hbuf[10 + k]
    head_out[...] = head

    own_r.wait()
    wait_recv(recv_r.at[pl.ds(0, 255)], 10)
    unpack(recv_r)
    for n in range(4):
        total = dot_tn(hot[0], collect(0, n))
        for s in range(1, 4):
            total += dot_tn(hot[s], collect(s, n))
        node_out[:, n * 256:(n + 1) * 256] = total

    wait_send(send_g.at[pl.ds(0, 255)], 2)
    wait_send(ft.at[:, :, pl.ds(0, 128)], 3)
    wait_send(at.at[:, :, pl.ds(0, 128)], 4)
    wait_send(d2.at[pl.ds(0, 128)], 5)
    wait_send(d1.at[pl.ds(0, 128)], 7)
    wait_send(ra, 8)
    wait_send(rb, 9)
    wait_send(send_r.at[pl.ds(0, 255)], 10)
    wait_send(r2a, 12)
    wait_send(r2b, 13)
    wait_send(r3a, 15)
    wait_send(r3b, 16)
    wait_send(hbuf.at[pl.ds(10, 7)], 17)


def shards(
    embeddings, endpoint_pairs, node_slot, first_weight, second_weight, score_weight, score_grad
):
    slots = node_slot[endpoint_pairs]
    owner = slots // ROWS
    local = slots - owner * ROWS
    oy, oz, oc, ox = owner // 64, (owner // 8) % 8, (owner // 4) % 2, owner % 4
    code = ((oy * 4 + ox) * 16 + oz * 2 + oc) * 512 + local
    vm = pl.BlockSpec(memory_space=pltpu.VMEM)
    hbm = pl.BlockSpec(memory_space=pl.ANY)
    V = pltpu.VMEM
    scratch = [
        V((ROWS, WIDTH), BF), V((2 * WIDTH, HID), BF), V((HID, HID), BF),
        V((NDEV, 2 * EDGES), jnp.int32), V((4, NDEV, ROWS), BF), V((2, NDEV * 16, 128), F32),
        V((NDEV, 16, 256), BF), V((NDEV, 16, 256), BF), V((NDEV, 16, 256), BF), V((NDEV, 16, 256), BF),
        V((EDGES, 2 * WIDTH), BF), V((EDGES, HID), BF), V((EDGES, HID), F32), V((EDGES, HID), BF),
        V((32, 2, 32, EDGES), BF), V((32, 32, 2 * EDGES), BF),
        V((32, 2, 16, EDGES), BF), V((32, 16, 2 * EDGES), BF),
        V((2 * EDGES, HID), BF), V((2 * EDGES, HID), BF), V((EDGES, 2 * WIDTH), BF),
        V((4, 4, 8, 16, 384), BF), V((4, 4, 8, 16, 384), BF),
        V((3, 4, 8, 16, 384), BF), V((3, 4, 8, 16, 384), BF),
        V((4, 8, 16, 384), BF), V((4, 8, 16, 384), BF),
        V((3, 8, 16, 384), BF), V((3, 8, 16, 384), BF),
        V((8, 16, 384), BF), V((8, 16, 384), BF),
        V((7, 16, 384), BF), V((7, 16, 384), BF),
        V((18, 1, HID), F32),
        V((15, 1, 2 * EDGES), jnp.int32),
        pltpu.SemaphoreType.DMA((5,)), pltpu.SemaphoreType.DMA((18,)), pltpu.SemaphoreType.DMA((18,)),
    ]
    score, node, first, second, head = pl.pallas_call(
        body,
        out_shape=(
            jax.ShapeDtypeStruct((1, EDGES), F32),
            jax.ShapeDtypeStruct((ROWS, WIDTH), F32),
            jax.ShapeDtypeStruct((8, HID), F32),
            jax.ShapeDtypeStruct((4, HID), F32),
            jax.ShapeDtypeStruct((1, HID), F32),
        ),
        in_specs=[vm] * 4 + [hbm] * 3,
        out_specs=(vm,) * 5,
        scratch_shapes=scratch,
        compiler_params=pltpu.CompilerParams(
            collective_id=0, has_side_effects=True, vmem_limit_bytes=56 * 2**20
        ),
    )(
        code.T.reshape(1, 2 * EDGES), code, score_grad.reshape(EDGES, 1), score_weight.reshape(1, HID),
        embeddings, first_weight, second_weight,
    )
    return score.reshape(EDGES), node, first, second, head.reshape(HID)


def solution(mesh):
    both = P(("dom", "rep"))
    rows = P(("dom", "rep"), None)
    return jax.shard_map(
        shards,
        mesh=mesh,
        in_specs=(rows, rows, P(), P(), P(), P(), both),
        out_specs=(both, rows, rows, rows, P()),
        check_vma=False,
    )
```

time: 1760 us -> 158 us (0.09)
  waiting for transfers between devices: 1320 us -> 0 us
  blocking collectives: 311 us -> 0 us
  Pallas kernels: 0 us -> 143 us
  local copies, waits for them, and re-layouts: 64.1 us -> 12 us
  matrix products: 17.9 us -> 0 us
    reduce_scatter x1 -> x0, waiting for transfers between devices: 1250 us -> none  [shards(): lax.psum_scatter(lax.dot_general(columns, first_delta, (((0,), (0,)), (()...]
    all_to_all x4 -> x0, blocking collectives: 197 us -> none  [the longest x1 109 us: shards(): lax.all_to_all(outgoing, 'dom', split_axis=0, concat_axis=0, tiled=True)]
    pallas_call x0 -> x1, Pallas kernels: none -> 143 us  [shards(): pl.pallas_call(body, out_shape=(jax.ShapeDtypeStruct((1, EDGES), F32), ja...]
    psum x1 -> x0, blocking collectives: 113 us -> none  [shards(): head_grad = lax.psum(head_local, ('dom', 'rep'))]
    unnamed x3 -> x0, waiting for transfers between devices: 44.8 us -> none
    all_to_all x2 -> x0, waiting for transfers between devices: 25.8 us -> none  [the longest x1 25.8 us: shards(): lax.all_to_all(lax.all_to_all(found, 'dom', split_axis=0, concat_axis=0,...]
    all_to_all x7 -> x0, local copies, waits for them, and re-layouts: 19.9 us -> none  [the longest x1 6.95 us: shards(): lax.all_to_all(lax.all_to_all(outgoing, 'dom', split_axis=0, concat_axis=...]
    dot_general x8 -> x0, matrix products: 17.9 us -> none  [the longest x1 4.51 us: shards(): lax.dot_general(columns, first_delta, (((0,), (0,)), ((), ())), preferred...]
  transfers between devices with their start and end apart: 4 -> 0, of which waited for: 3 -> 0; matrix products, arithmetic and copies ran while one was open for 3% -> 0% of each run, Pallas kernels for 0% -> 0%
where the time goes in v1:
time: 158 us
  Pallas kernels  143 us (91%)
  local copies, waits for them, and re-layouts  12 us (8%)
  other arithmetic  2.51 us (2%)
    pallas_call x1, Pallas kernels, shards(): pl.pallas_call(body, out_shape=(jax.ShapeDtypeStruct((1, EDGES), F32), ja...  143 us
    unnamed x14, local copies, waits for them, and re-layouts  6.5 us

profile of v1, /device:TPU:1, one launch (start us, length us, event | category | flops | bytes accessed | tf_op | source)
XLA Modules:
  0.0 157.9 jit_solution(7680350973731156764)
XLA Ops:
  0.6 0.0 copy-start
  0.6 0.7 broadcast_compare_fusion
  1.4 0.7 broadcast_add_fusion
  2.1 1.3 reshape.27.sw_row
  3.3 0.1 copy.26
  3.5 0.1 copy.27
  3.6 1.4 copy.30.sgrad_col
  5.0 0.8 copy.28
  5.8 0.1 reshape.32
  5.9 0.0 copy-done
  5.9 1.7 %gather_fusion = s32[256]{0:T(256)S(1)} fusion(s32[98304]{0:T(1024)S(1)} %copy-done, s32[1024]{0:T(1024)S(1)} %pad_clamp_fusion), kind=kCustom, calls=%fused_computation | custom fusion | bytes 3072 | tf_op jit(solution)/shard_map/gather | solution.py:379
  7.7 0.1 reshape.31
  7.8 0.2 fusion.7
  8.0 0.6 copy.29
  8.7 0.9 fusion.19.code_col
  9.5 142.6 %shard_map.110 = (f32[1,128]{1,0:T(1,128)}, f32[384,1024]{1,0:T(8,128)}, f32[8,1024]{1,0:T(8,128)}, f32[4,1024]{1,0:T(4,128)}, f32[1,1024]{1,0:T(1,128)}) custom-call(s32[1,256]{1,0:T(1,128)} %bitcast.25, s32[128,2]{1,0:T(8,128)} %fusion.19.code_col, f32[128,1]{1,0:T(8,128)} %copy.30.sgrad_col, bf16[1,1024]{1,0:T(2,128)(2,1)} %reshape.27.sw_row, ...), custom_call_target="tpu_custom_call" | custom-call | tf_op jit(solution)/shard_map/pallas_call | solution.py:405
  152.1 0.0 copy-start.1
  152.2 0.0 copy-start.2
  152.2 0.0 copy-start.3
  152.2 1.2 copy.36
  153.3 2.7 %copy.37 = f32[384,1024]{1,0:T(8,128)} copy(f32[384,1024]{1,0:T(8,128)} %get-tuple-element.21) | data formatting | bytes 3145728
  156.1 0.0 copy-done.1
  156.1 0.6 copy.38
  156.7 0.0 copy-done.2
  156.7 0.6 copy.39
  157.3 0.0 copy-done.3
  157.3 0.6 copy.40
  (2 shorter events, 0.0 us)
Async XLA Ops:
  0.6 5.3 %copy-start = (s32[98304]{0:T(1024)S(1)}, s32[98304]{0:T(1024)}, u32[]{:S(2)}) copy-start(s32[98304]{0:T(1024)} %param.9) | copy-start | bytes 1179652
  152.1 3.9 %copy-start.1 = (f32[8,1024]{1,0:T(8,128)S(1)}, f32[8,1024]{1,0:T(8,128)}, u32[]{:S(2)}) copy-start(f32[8,1024]{1,0:T(8,128)} %get-tuple-element.22) | copy-start | bytes 98308
  152.2 4.5 %copy-start.2 = (f32[4,1024]{1,0:T(4,128)S(1)}, f32[4,1024]{1,0:T(4,128)}, u32[]{:S(2)}) copy-start(f32[4,1024]{1,0:T(4,128)} %get-tuple-element.23) | copy-start | bytes 49156
  152.2 5.1 %copy-start.3 = (f32[1,1024]{1,0:T(1,128)S(1)}, f32[1,1024]{1,0:T(1,128)}, u32[]{:S(2)}) copy-start(f32[1,1024]{1,0:T(1,128)} %get-tuple-element.14) | copy-start | bytes 12292

commit v2 on v1

v2 whole, which is shorter than its diff:
```python
import functools

import jax
import jax.numpy as jnp
from jax import lax
from jax.experimental import pallas as pl
from jax.experimental.pallas import tpu as pltpu
from jax.sharding import PartitionSpec as P

MESH = pl.DeviceIdType.MESH
NY, NZ, NC, NX = 4, 8, 2, 4
NZC, NXY = NZ * NC, NX * NY
NDEV = NZC * NXY
NODES = 98304
ROWS, WIDTH, HID, EDGES = 384, 1024, 1024, 128
BF, F32 = jnp.bfloat16, jnp.float32
GELU_A, GELU_B = 0.7978845608028654, 0.044715


def dot(a, b):
    return jnp.dot(a, b, preferred_element_type=F32)


def dot_nt(a, b):
    return lax.dot_general(a, b, (((1,), (1,)), ((), ())), preferred_element_type=F32)


def dot_tn(a, b):
    return lax.dot_general(a, b, (((0,), (0,)), ((), ())), preferred_element_type=F32)


def gelu_both(v):
    t = jnp.tanh(GELU_A * (v + GELU_B * (v * v * v)))
    half = 0.5 * (1.0 + t)
    slope = half + 0.5 * v * (1.0 - t * t) * (GELU_A * (1.0 + (3.0 * GELU_B) * (v * v)))
    return v * half, slope


def iota(shape, dim):
    return lax.broadcasted_iota(jnp.int32, shape, dim)


def body(
    pairs, sgrad_in, sw_in, table_hbm, emb_hbm, w1_hbm, w2_hbm,
    node_out, small_out,
    table, emb, w1, w2, w1t, w2t, idx, hot, hot_t, picks, picks_t, stage,
    send_g, recv_g, send_r, recv_r,
    feats, first_act, first_slope, ft_own, ft, at_own, at, d1, d2, fg,
    pa, pb, ra, rb, ua, ub, sa, sb, r2a, r2b, ta, tb, r3a, r3b, hbuf,
    fifteen, load_sem, ss, rs,
):
    dom = lax.axis_index("dom")
    x = lax.axis_index("rep")
    y, z, c = dom // 16, (dom // 2) % 8, dom % 2
    zc = z * 2 + c
    xy = y * 4 + x
    me = xy * 16 + zc

    def ident(yy, zz, cc, xx):
        return ((yy * 8 + zz) * 2 + cc, xx)

    def zc_peer(k):
        return ident(y, (z + k % 8) % 8, (c + k // 8) % 2, x)

    def xy_peer(k):
        return ident((y + k // 4) % 4, z, c, (x + k % 4) % 4)

    def rcopy(src, dst, sem, dev):
        return pltpu.make_async_remote_copy(
            src_ref=src, dst_ref=dst, send_sem=ss.at[sem], recv_sem=rs.at[sem],
            device_id=dev, device_id_type=MESH,
        )

    def wait_send(ref, sem):
        pltpu.make_async_copy(ref, ref, ss.at[sem]).wait()

    def wait_recv(ref, sem):
        pltpu.make_async_copy(ref, ref, rs.at[sem]).wait()

    loads = [
        pltpu.make_async_copy(table_hbm, table, load_sem.at[0]),
        pltpu.make_async_copy(emb_hbm, emb, load_sem.at[1]),
        pltpu.make_async_copy(w1_hbm, w1, load_sem.at[2]),
        pltpu.make_async_copy(w2_hbm, w2, load_sem.at[3]),
    ]
    for load in loads:
        load.start()
    bar = pltpu.get_barrier_semaphore()

    for k in range(1, 16):
        pl.semaphore_signal(bar, inc=1, device_id=zc_peer(k), device_id_type=MESH)
        pl.semaphore_signal(bar, inc=1, device_id=xy_peer(k), device_id_type=MESH)

    eye = iota((128, 128), 0) == iota((128, 128), 1)
    lanes = iota((128, 128), 1)
    loads[0].wait()
    slots = table[...]
    digits = jnp.concatenate(
        [(slots & 255).astype(F32), ((slots >> 8) & 255).astype(F32), (slots >> 16).astype(F32)], axis=1
    ).astype(BF)
    col_code, row_code = [], []
    for side in range(2):
        node_id = pairs[side:side + 1, :].astype(F32)
        node_id = jnp.sum(jnp.where(eye, node_id, 0.0), axis=1, keepdims=True).astype(jnp.int32)
        rows = ((node_id >> 7) == iota((128, NODES // 128), 1)).astype(F32).astype(BF)
        got = dot(rows, digits)
        slot = got[:, 0:128] + 256.0 * got[:, 128:256] + 65536.0 * got[:, 256:384]
        slot = jnp.sum(jnp.where(lanes == (node_id & 127), slot, 0.0), axis=1, keepdims=True)
        owner = ((slot + 0.5) * (1.0 / ROWS)).astype(jnp.int32)
        local = slot.astype(jnp.int32) - owner * ROWS
        quick = ((owner >> 6) * 4 + (owner & 3)) * 16 + ((owner >> 2) & 15)
        code = quick * 512 + local
        row = jnp.sum(jnp.where(eye, code.astype(F32), 0.0), axis=0, keepdims=True).astype(jnp.int32)
        col_code.append(code)
        row_code.append(row)

    idx[pl.ds(me, 1), :] = jnp.concatenate(row_code, axis=1)
    pl.semaphore_wait(bar, 30)

    for k in range(1, 16):
        row = idx.at[pl.ds(me, 1)]
        rcopy(row, row, 0, zc_peer(k)).start()

    wait_recv(fifteen, 0)

    for k in range(1, 16):
        rows = idx.at[pl.ds(xy * 16, 16)]
        rcopy(rows, rows, 1, xy_peer(k)).start()

    wait_recv(idx.at[pl.ds(0, 240)], 1)

    before = (iota((128, 128), 0) < iota((128, 128), 1)).astype(F32).astype(BF)
    for side in range(2):
        codes = idx[:, side * 128:(side + 1) * 128]
        mine = (codes >> 9) == me
        rank = dot(mine.astype(F32).astype(BF), before)
        local = ((codes & 511) + 1).astype(F32)
        for k in range(2):
            s = side * 2 + k
            hit = mine & (rank == float(k))
            found = jnp.sum(jnp.where(hit, local, 0.0), axis=1, keepdims=True).astype(jnp.int32) - 1
            for b in range(4):
                hot[b, s * 64:(s + 1) * 64, :] = (
                    (found[b * 64:(b + 1) * 64] == iota((64, ROWS), 1)).astype(F32).astype(BF)
                )

    def spread(s, n, part):
        for h in range(2):
            stage[h, pl.ds(s * 4 + n, 64, stride=16), :] = part[:, h * 128:(h + 1) * 128]

    def pack(dst, b):
        @pl.loop(0, 4)
        def _(i):
            rows = pl.ds(i * 256, 256)
            both = jnp.concatenate([stage[0, rows, :], stage[1, rows, :]], axis=1)
            dst[pl.ds(b * 64 + i * 16, 16)] = both.astype(BF).reshape(16, 16, 256)

    def unpack(src, b):
        @pl.loop(0, 4)
        def _(i):
            rows = pl.ds(i * 256, 256)
            both = src[pl.ds(b * 64 + i * 16, 16)].reshape(256, 256).astype(F32)
            stage[0, rows, :] = both[:, :128]
            stage[1, rows, :] = both[:, 128:]

    def collect(ss, n):
        out = []
        for s in ss:
            rows = pl.ds(s * 4 + n, 64, stride=16)
            out.append(jnp.concatenate([stage[0, rows, :], stage[1, rows, :]], axis=1))
        return jnp.concatenate(out, axis=0).astype(BF)

    def send_block(src, dst, j, sem):
        yy = (y + j) % 4

        @pl.loop(0, 8)
        def _(k):
            xx = (x + k % 4) % 4
            cc = (c + k // 4) % 2

            def push(zz):
                to = (yy * 4 + xx) * 16 + zz * 2 + cc
                rcopy(src.at[to], dst.at[me], sem + j, ident(yy, zz, cc, xx)).start()

            @pl.when(j + k > 0)
            def _():
                push(z)

            for i in range(1, 8):
                push((z + i) % 8)

    def wait_block(dst, j, sem):
        @pl.when(j == 0)
        def _():
            wait_recv(dst.at[pl.ds(0, 63)], sem)

        @pl.when(j > 0)
        def _():
            wait_recv(dst.at[pl.ds(0, 64)], sem + j)

    def wait_block_sent(src, sem):
        wait_send(src.at[pl.ds(0, 63)], sem)
        for j in range(1, 4):
            wait_send(src.at[pl.ds(0, 64)], sem + j)

    G, R = 2, 6
    loads[1].wait()

    @pl.loop(0, 4)
    def _(j):
        b = (y + j) % 4
        for n in range(4):
            part = dot(hot[b], emb[:, n * 256:(n + 1) * 256])
            for s in range(4):
                spread(s, n, part[s * 64:(s + 1) * 64])
        pack(send_g, b)
        send_block(send_g, recv_g, j, G)

    recv_g[me] = send_g[me]

    earlier = iota((128, 128), 1) < iota((128, 128), 0)
    for side in range(2):
        row_owner = row_code[side] >> 9
        col_owner = col_code[side] >> 9
        rank = jnp.sum(jnp.where((col_owner == row_owner) & earlier, 1.0, 0.0), axis=1, keepdims=True)
        for b in range(4):
            home = col_owner == b * 64 + (lanes & 63)
            pick = jnp.where(home & (rank == (lanes >> 6).astype(F32)), 1.0, 0.0)
            picks[b, side] = pick.astype(BF)
            picks_t[b, side] = pick.T.astype(BF)
    feats[...] = jnp.zeros_like(feats)

    @pl.loop(0, 4)
    def _(b):
        hot_t[b] = hot[b].T

    loads[2].wait()
    loads[3].wait()

    @pl.loop(0, 8)
    def _(i):
        rows = pl.ds(pl.multiple_of(i * 256, 256), 256)
        for n in range(4):
            w1t[n * 256:(n + 1) * 256, rows] = w1[rows, n * 256:(n + 1) * 256].T

    @pl.loop(0, 4)
    def _(i):
        rows = pl.ds(pl.multiple_of(i * 256, 256), 256)
        for n in range(4):
            w2t[n * 256:(n + 1) * 256, rows] = w2[rows, n * 256:(n + 1) * 256].T

    @pl.loop(0, 4)
    def _(j):
        b = (y + 4 - j) % 4
        wait_block(recv_g, j, G)
        unpack(recv_g, b)
        for side in range(2):
            for n in range(4):
                cols = slice(side * 1024 + n * 256, side * 1024 + (n + 1) * 256)
                part = dot(picks[b, side], collect((side * 2, side * 2 + 1), n))
                feats[:, cols] = feats[:, cols] + part.astype(BF)

    other = ident(y, z, 1 - c, x)
    for n in range(4):
        cols = slice(n * 256, (n + 1) * 256)
        act, slope = gelu_both(dot(feats[...], w1[:, cols]))
        act = act.astype(BF)
        first_act[:, cols] = act
        first_slope[:, cols] = slope

    score = jnp.zeros((1, 128), F32)
    sgrad = jnp.sum(jnp.where(eye, sgrad_in[...], 0.0), axis=1, keepdims=True)
    for n in range(4):
        cols = slice(n * 256, (n + 1) * 256)
        act, slope = gelu_both(dot(first_act[...], w2[:, cols]))
        act = act.astype(BF)
        sw = sw_in[cols].reshape(1, 256)
        score += dot_nt(jnp.broadcast_to(sw, (8, 256)), act)[0:1]
        hbuf[0, :, cols] = jnp.sum(sgrad * act.astype(F32), axis=0, keepdims=True)
        d2[0:128, cols] = (sgrad * sw.astype(F32) * slope).astype(BF)
    small_out[13:14, 0:128] = score
    rcopy(d2.at[pl.ds(0, 128)], d2.at[pl.ds(128, 128)], 12, other).start()
    rcopy(hbuf.at[0], hbuf.at[1], 13, other).start()

    for n in range(4):
        cols = slice(n * 256, (n + 1) * 256)
        back = dot(d2[0:128, :], w2t[:, cols])
        d1[0:128, cols] = (back * first_slope[:, cols]).astype(BF)
    rcopy(d1.at[pl.ds(0, 128)], d1.at[pl.ds(128, 128)], 14, other).start()

    for n in range(8):
        cols = slice(n * 256, (n + 1) * 256)
        fg[:, cols] = dot(d1[0:128, :], w1t[:, cols]).astype(BF)

    def return_block(j):
        b = (y + j) % 4
        for side in range(2):
            for n in range(4):
                col = side * 1024 + n * 256
                part = dot(picks_t[b, side], fg[:, col:col + 256])
                for k in range(2):
                    spread(side * 2 + k, n, part[k * 64:(k + 1) * 64])
        pack(send_r, b)
        send_block(send_r, recv_r, j, R)

    @pl.loop(0, 1)
    def _(j):
        return_block(j)

    for i in range(4):
        cols = slice(i * 256, (i + 1) * 256)
        at_own[i * 8:(i + 1) * 8] = first_act[:, cols].T.reshape(8, 2, 16, 128)
    rcopy(at_own.at[:, 1 - c], at.at[:, :, pl.ds(128, 128)], 11, other).start()
    at[:, :, 0:128] = at_own[:, c]
    for i in range(8):
        cols = slice(i * 256, (i + 1) * 256)
        ft_own[i * 4:(i + 1) * 4] = feats[:, cols].T.reshape(4, 2, 32, 128)
    rcopy(ft_own.at[:, 1 - c], ft.at[:, :, pl.ds(128, 128)], 10, other).start()
    ft[:, :, 0:128] = ft_own[:, c]

    wait_recv(at.at[:, :, pl.ds(0, 128)], 11)
    wait_recv(d2.at[pl.ds(0, 128)], 12)
    low = iota((8, 8, 512), 1) < 4

    @pl.loop(0, 4)
    def _(yy):
        res = dot(at[pl.ds(yy * 8, 8)].reshape(128, 256), d2[...]).reshape(8, 16, 1024)
        for pair in range(2):
            lo = res[:, pair * 8:(pair + 1) * 8, :512]
            hi = res[:, pair * 8:(pair + 1) * 8, 512:]
            even = jnp.where(low, lo, pltpu.roll(hi, 4, axis=1))
            odd = jnp.where(low, pltpu.roll(lo, 4, axis=1), hi)
            for bit, part in ((0, even), (1, odd)):
                full = jnp.concatenate([part[:, :, :256], part[:, :, 256:]], axis=1)
                pb[yy, pair * 2 + bit, :, :, 128:384] = full.astype(BF)

    wait_recv(ft.at[:, :, pl.ds(0, 128)], 10)
    wait_recv(d1.at[pl.ds(0, 128)], 14)

    @pl.loop(0, 4)
    def _(yy):
        lhs = ft[pl.ds(yy * 8, 8)].reshape(256, 256)
        for n in range(2):
            lo = dot(lhs, d1[:, n * 256:(n + 1) * 256]).reshape(8, 4, 8, 256)
            hi = dot(lhs, d1[:, 512 + n * 256:512 + (n + 1) * 256]).reshape(8, 4, 8, 256)
            for xx in range(4):
                full = jnp.concatenate([lo[:, xx], hi[:, xx]], axis=1).astype(BF)
                if n == 0:
                    pa[xx, yy, :, :, 0:256] = full
                else:
                    pa[xx, yy, :, :, 256:384] = full[:, :, :128]
                    pb[yy, xx, :, :, 0:128] = full[:, :, 128:]

    def along(axis, k):
        if axis == "x":
            return ident(y, z, c, (x + k) % 4), (x + k) % 4
        if axis == "y":
            return ident((y + k) % 4, z, c, x), (y + k) % 4
        return ident(y, (z + k) % 8, c, x), (z + k) % 8

    near, far = pl.ds(0, 2), pl.ds(2, 2)
    for axis, mine, buf, got, aug, sem in (("x", x, pa, ra, ua, 15), ("y", y, pb, rb, ub, 16)):
        right, to_right = along(axis, 1)
        left, to_left = along(axis, 3)
        opposite = (mine + 2) % 4
        rcopy(buf.at[opposite, near], aug.at[0], sem + 9, right).start()
        rcopy(buf.at[opposite, far], aug.at[1], sem + 9, left).start()
        rcopy(buf.at[to_right, far], got.at[0, far], sem, right).start()
        rcopy(buf.at[to_left, near], got.at[1, near], sem, left).start()
    @pl.loop(1, 2)
    def _(j):
        return_block(j)

    for axis, mine, buf, got, aug, sem in (("x", x, pa, ra, ua, 15), ("y", y, pb, rb, ub, 16)):
        right, to_right = along(axis, 1)
        left, to_left = along(axis, 3)
        wait_recv(aug, sem + 9)

        @pl.loop(0, 2)
        def _(i):
            buf[to_right, i] = (buf[to_right, i].astype(F32) + aug[0, i].astype(F32)).astype(BF)
            buf[to_left, 2 + i] = (buf[to_left, 2 + i].astype(F32) + aug[1, i].astype(F32)).astype(BF)

        rcopy(buf.at[to_right, near], got.at[0, near], sem, right).start()
        rcopy(buf.at[to_left, far], got.at[1, far], sem, left).start()

    @pl.loop(2, 4)
    def _(j):
        return_block(j)

    recv_r[me] = send_r[me]

    def head_step(base, count, axis, mine, sem):
        for k in range(1, count):
            dev, _ = along(axis, k)
            rcopy(hbuf.at[base + mine], hbuf.at[base + mine], sem, dev).start()

    wait_recv(hbuf.at[0], 13)
    wait_send(hbuf.at[0], 13)
    hbuf[2 + x] = hbuf[0] + hbuf[1]
    head_step(2, 4, "x", x, 17)

    def add3(own, got, out, sec):
        total = own[sec].astype(F32) + got[0, sec].astype(F32) + got[1, sec].astype(F32)
        out[sec] = total.astype(BF)

    node_out[...] = jnp.zeros_like(node_out)

    def land_block(j):
        b = (y + 4 - j) % 4
        wait_block(recv_r, j, R)
        unpack(recv_r, b)
        for n in range(4):
            cols = slice(n * 256, (n + 1) * 256)
            node_out[:, cols] = node_out[:, cols] + dot(hot_t[b], collect((0, 1, 2, 3), n))

    wait_recv(ra, 15)

    @pl.loop(0, 4)
    def _(i):
        add3(pa.at[x], ra, sa, i)

    for k in range(1, 4):
        dev, at_y = along("y", k)
        rcopy(sa.at[at_y], r2a.at[k - 1], 18, dev).start()
    wait_recv(rb, 16)

    @pl.loop(0, 4)
    def _(i):
        add3(pb.at[y], rb, sb, i)

    for k in range(1, 4):
        dev, at_x = along("x", k)
        rcopy(sb.at[at_x], r2b.at[k - 1], 19, dev).start()

    @pl.loop(0, 1)
    def _(j):
        land_block(j)

    wait_recv(hbuf.at[pl.ds(2, 3)], 17)
    wait_send(hbuf.at[pl.ds(2, 3)], 17)
    hbuf[6 + y] = hbuf[2] + hbuf[3] + hbuf[4] + hbuf[5]
    head_step(6, 4, "y", y, 20)

    wait_recv(r2a, 18)
    total = sa[y].astype(F32) + r2a[0].astype(F32) + r2a[1].astype(F32) + r2a[2].astype(F32)
    ta[...] = total.astype(BF)
    for k in range(1, 8):
        dev, at_z = along("z", k)
        rcopy(ta.at[at_z], r3a.at[k - 1], 21, dev).start()
    wait_recv(r2b, 19)
    total = sb[x].astype(F32) + r2b[0].astype(F32) + r2b[1].astype(F32) + r2b[2].astype(F32)
    tb[...] = total.astype(BF)
    for k in range(1, 8):
        dev, at_z = along("z", k)
        rcopy(tb.at[at_z], r3b.at[k - 1], 22, dev).start()

    wait_recv(hbuf.at[pl.ds(6, 3)], 20)
    wait_send(hbuf.at[pl.ds(6, 3)], 20)
    hbuf[10 + z] = hbuf[6] + hbuf[7] + hbuf[8] + hbuf[9]
    head_step(10, 8, "z", z, 23)

    @pl.loop(1, 3)
    def _(j):
        land_block(j)

    wait_recv(r3a, 21)
    wait_recv(r3b, 22)
    left = ta[z].astype(F32)
    right = tb[z].astype(F32)
    for k in range(7):
        left += r3a[k].astype(F32)
        right += r3b[k].astype(F32)
    whole = jnp.concatenate([left, right], axis=1)
    small_out[0:8, 0:512] = whole[0:8, 0:512]
    small_out[0:8, 512:1024] = whole[8:16, 0:512]
    small_out[8:12, 0:256] = whole[0:4, 512:768]
    small_out[8:12, 512:768] = whole[4:8, 512:768]
    small_out[8:12, 256:512] = whole[8:12, 512:768]
    small_out[8:12, 768:1024] = whole[12:16, 512:768]

    wait_recv(hbuf.at[pl.ds(10, 7)], 23)
    head = hbuf[10]
    for k in range(1, 8):
        head += hbuf[10 + k]
    small_out[12:13, :] = head

    @pl.loop(3, 4)
    def _(j):
        land_block(j)

    wait_send(fifteen, 0)
    wait_send(idx.at[pl.ds(0, 240)], 1)
    wait_block_sent(send_g, G)
    wait_block_sent(send_r, R)
    wait_send(ft.at[:, :, pl.ds(0, 128)], 10)
    wait_send(at.at[:, :, pl.ds(0, 128)], 11)
    wait_send(d2.at[pl.ds(0, 128)], 12)
    wait_send(d1.at[pl.ds(0, 128)], 14)
    wait_send(ra, 15)
    wait_send(rb, 16)
    wait_send(ua, 24)
    wait_send(ub, 25)
    wait_send(r2a, 18)
    wait_send(r2b, 19)
    wait_send(r3a, 21)
    wait_send(r3b, 22)
    wait_send(hbuf.at[pl.ds(10, 7)], 23)


def deliver(node_in, small_in, score_out, node_out, first_out, second_out, head_out, held, small, sem_in, sem_out):
    spans = [pl.ds(i * 96, 96) for i in range(4)]
    ins = [pltpu.make_async_copy(node_in.at[p], held.at[p], sem_in.at[i]) for i, p in enumerate(spans)]
    outs = [pltpu.make_async_copy(held.at[p], node_out.at[p], sem_out.at[i]) for i, p in enumerate(spans)]
    rest = pltpu.make_async_copy(small_in, small, sem_in.at[4])
    for copy in ins + [rest]:
        copy.start()
    for i in range(4):
        ins[i].wait()
        outs[i].start()
    rest.wait()
    score_out[...] = small[13:14, 0:128].reshape(128)
    first_out[...] = small[0:8, :]
    second_out[...] = small[8:12, :]
    head_out[...] = small[12:13, :].reshape(HID)
    for copy in outs:
        copy.wait()


def shards(
    embeddings, endpoint_pairs, node_slot, first_weight, second_weight, score_weight, score_grad
):
    vm = pl.BlockSpec(memory_space=pltpu.VMEM)
    hbm = pl.BlockSpec(memory_space=pltpu.HBM)
    V = pltpu.VMEM
    scratch = [
        V((NODES // 128, 128), jnp.int32), V((ROWS, WIDTH), BF), V((2 * WIDTH, HID), BF), V((HID, HID), BF),
        V((HID, 2 * WIDTH), BF), V((HID, HID), BF),
        V((NDEV, 2 * EDGES), jnp.int32), V((4, NDEV, ROWS), BF), V((4, ROWS, NDEV), BF),
        V((4, 2, EDGES, 128), BF), V((4, 2, 128, EDGES), BF), V((2, 64 * 16, 128), F32),
        V((NDEV, 16, 256), BF), V((NDEV, 16, 256), BF), V((NDEV, 16, 256), BF), V((NDEV, 16, 256), BF),
        V((EDGES, 2 * WIDTH), BF), V((EDGES, HID), BF), V((EDGES, HID), F32),
        V((32, 2, 32, EDGES), BF), V((32, 32, 2 * EDGES), BF),
        V((32, 2, 16, EDGES), BF), V((32, 16, 2 * EDGES), BF),
        V((2 * EDGES, HID), BF), V((2 * EDGES, HID), BF), V((EDGES, 2 * WIDTH), BF),
        V((4, 4, 8, 16, 384), BF), V((4, 4, 8, 16, 384), BF),
        V((2, 4, 8, 16, 384), BF), V((2, 4, 8, 16, 384), BF),
        V((2, 2, 8, 16, 384), BF), V((2, 2, 8, 16, 384), BF),
        V((4, 8, 16, 384), BF), V((4, 8, 16, 384), BF),
        V((3, 8, 16, 384), BF), V((3, 8, 16, 384), BF),
        V((8, 16, 384), BF), V((8, 16, 384), BF),
        V((7, 16, 384), BF), V((7, 16, 384), BF),
        V((18, 1, HID), F32),
        V((15, 1, 2 * EDGES), jnp.int32),
        pltpu.SemaphoreType.DMA((4,)), pltpu.SemaphoreType.DMA((26,)), pltpu.SemaphoreType.DMA((26,)),
    ]
    node, small = pl.pallas_call(
        body,
        out_shape=(
            jax.ShapeDtypeStruct((ROWS, WIDTH), F32),
            jax.ShapeDtypeStruct((16, HID), F32),
        ),
        in_specs=[vm] * 3 + [hbm] * 4,
        out_specs=(vm, vm),
        scratch_shapes=scratch,
        compiler_params=pltpu.CompilerParams(
            collective_id=0, has_side_effects=True, vmem_limit_bytes=58 * 2**20
        ),
    )(
        endpoint_pairs.T, score_grad.reshape(1, EDGES), score_weight,
        node_slot.reshape(NODES // 128, 128), embeddings, first_weight, second_weight,
    )
    return pl.pallas_call(
        deliver,
        out_shape=(
            jax.ShapeDtypeStruct((EDGES,), F32),
            jax.ShapeDtypeStruct((ROWS, WIDTH), F32),
            jax.ShapeDtypeStruct((8, HID), F32),
            jax.ShapeDtypeStruct((4, HID), F32),
            jax.ShapeDtypeStruct((HID,), F32),
        ),
        in_specs=[hbm, hbm],
        out_specs=(vm, hbm, vm, vm, vm),
        scratch_shapes=[
            V((ROWS, WIDTH), F32), V((16, HID), F32), pltpu.SemaphoreType.DMA((5,)), pltpu.SemaphoreType.DMA((4,)),
        ],
    )(node, small)


def solution(mesh):
    both = P(("dom", "rep"))
    rows = P(("dom", "rep"), None)
    return jax.shard_map(
        shards,
        mesh=mesh,
        in_specs=(rows, rows, P(), P(), P(), P(), both),
        out_specs=(both, rows, rows, rows, P()),
        check_vma=False,
    )
```

time: 158 us -> 140 us (0.89)
  local copies, waits for them, and re-layouts: 12 us -> 0 us
  Pallas kernels: 143 us -> 139 us
  other arithmetic: 2.51 us -> 0 us
    unnamed x14 -> x0, local copies, waits for them, and re-layouts: 6.5 us -> none
    pallas_call x1 -> x2, Pallas kernels: 143 us -> 139 us  [the longest x1 137 us: shards(): pl.pallas_call(body, out_shape=(jax.ShapeDtypeStruct((ROWS, WIDTH), F32),...]
    reshape x2 -> x0, local copies, waits for them, and re-layouts: 2.65 us -> none  [the longest x1 1.38 us: shards(): score_grad.reshape(EDGES, 1)]
    gather x2 -> x0, local copies, waits for them, and re-layouts: 1.86 us -> none  [shards(): slots = node_slot[endpoint_pairs]]
    add x3 -> x0, other arithmetic: 1.76 us -> none  [the longest x2 1.08 us: shards(): code = ((oy * 4 + ox) * 16 + oz * 2 + oc) * 512 + local]
where the time goes in v2:
time: 140 us
  Pallas kernels  139 us (99%)
    pallas_call x1, Pallas kernels, shards(): pl.pallas_call(body, out_shape=(jax.ShapeDtypeStruct((ROWS, WIDTH), F32),...  137 us
    pallas_call x1, Pallas kernels, shards(): pl.pallas_call(deliver, out_shape=(jax.ShapeDtypeStruct((EDGES,), F32), j...  2.83 us

profile of v2, /device:TPU:1, one launch (start us, length us, event | category | flops | bytes accessed | tf_op | source)
XLA Modules:
  0.0 140.1 jit_solution(7205272775791680093)
XLA Ops:
  0.6 136.6 %shard_map.110 = (f32[384,1024]{1,0:T(8,128)}, f32[16,1024]{1,0:T(8,128)}) custom-call(s32[2,128]{1,0:T(2,128)} %bitcast.4, f32[1,128]{1,0:T(1,128)} %bitcast.5, bf16[1024]{0:T(1024)(128)(2,1)} %sw_in.1, s32[768,128]{1,0:T(8,128)} %bitcast.3, bf16[384,1024]{1,0:T(8,128)(2,1)} %emb_hbm.1, bf16[2048,1024]{1,0:T(8,128)(2,1)} %w1_hbm.1, bf16[1024,1024]{1,0:T(8,128)(2,1)} %w2_hbm.1), custom_call_target="tpu_custom_call" | custom-call | tf_op jit(solution)/shard_map/pallas_call | solution.py:557
  137.2 2.8 %shard_map.111 = (f32[128]{0:T(128)}, f32[384,1024]{1,0:T(8,128)}, f32[8,1024]{1,0:T(8,128)}, f32[4,1024]{1,0:T(4,128)}, f32[1024]{0:T(1024)}) custom-call(f32[384,1024]{1,0:T(8,128)} %get-tuple-element.7.node_in, f32[16,1024]{1,0:T(8,128)} %get-tuple-element.8.small_in), custom_call_target="tpu_custom_call" | custom-call | tf_op jit(solution)/shard_map/pallas_call | solution.py:573

commit v3 on v2

--- a/solution.py
+++ b/solution.py
@@ -83,8 +83,7 @@
         pltpu.make_async_copy(w1_hbm, w1, load_sem.at[2]),
         pltpu.make_async_copy(w2_hbm, w2, load_sem.at[3]),
     ]
-    for load in loads:
-        load.start()
+    loads[0].start()
     bar = pltpu.get_barrier_semaphore()
 
     for k in range(1, 16):
@@ -94,6 +93,8 @@
     eye = iota((128, 128), 0) == iota((128, 128), 1)
     lanes = iota((128, 128), 1)
     loads[0].wait()
+    for load in loads[1:]:
+        load.start()
     slots = table[...]
     digits = jnp.concatenate(
         [(slots & 255).astype(F32), ((slots >> 8) & 255).astype(F32), (slots >> 16).astype(F32)], axis=1
@@ -170,10 +171,10 @@
             out.append(jnp.concatenate([stage[0, rows, :], stage[1, rows, :]], axis=1))
         return jnp.concatenate(out, axis=0).astype(BF)
 
-    def send_block(src, dst, j, sem):
+    def send_block(src, dst, j, sem, first=0, last=8):
         yy = (y + j) % 4
 
-        @pl.loop(0, 8)
+        @pl.loop(first, last)
         def _(k):
             xx = (x + k % 4) % 4
             cc = (c + k // 4) % 2
@@ -292,7 +293,7 @@
         cols = slice(n * 256, (n + 1) * 256)
         fg[:, cols] = dot(d1[0:128, :], w1t[:, cols]).astype(BF)
 
-    def return_block(j):
+    def return_pack(j):
         b = (y + j) % 4
         for side in range(2):
             for n in range(4):
@@ -301,11 +302,14 @@
                 for k in range(2):
                     spread(side * 2 + k, n, part[k * 64:(k + 1) * 64])
         pack(send_r, b)
-        send_block(send_r, recv_r, j, R)
-
-    @pl.loop(0, 1)
-    def _(j):
-        return_block(j)
+
+    def groups(first, last):
+        for i in range(first, last):
+            if i % 4 == 0:
+                return_pack(i // 4)
+            send_block(send_r, recv_r, i // 4, R, i % 4 * 2, i % 4 * 2 + 2)
+
+    groups(0, 2)
 
     for i in range(4):
         cols = slice(i * 256, (i + 1) * 256)
@@ -359,7 +363,8 @@
         return ident(y, (z + k) % 8, c, x), (z + k) % 8
 
     near, far = pl.ds(0, 2), pl.ds(2, 2)
-    for axis, mine, buf, got, aug, sem in (("x", x, pa, ra, ua, 15), ("y", y, pb, rb, ub, 16)):
+    stages = (("x", x, pa, ra, ua, 15), ("y", y, pb, rb, ub, 16))
+    for axis, mine, buf, got, aug, sem in stages:
         right, to_right = along(axis, 1)
         left, to_left = along(axis, 3)
         opposite = (mine + 2) % 4
@@ -367,11 +372,20 @@
         rcopy(buf.at[opposite, far], aug.at[1], sem + 9, left).start()
         rcopy(buf.at[to_right, far], got.at[0, far], sem, right).start()
         rcopy(buf.at[to_left, near], got.at[1, near], sem, left).start()
-    @pl.loop(1, 2)
-    def _(j):
-        return_block(j)
-
-    for axis, mine, buf, got, aug, sem in (("x", x, pa, ra, ua, 15), ("y", y, pb, rb, ub, 16)):
+
+    def head_step(base, count, axis, mine, sem):
+        for k in range(1, count):
+            dev, _ = along(axis, k)
+            rcopy(hbuf.at[base + mine], hbuf.at[base + mine], sem, dev).start()
+
+    wait_recv(hbuf.at[0], 13)
+    wait_send(hbuf.at[0], 13)
+    hbuf[2 + x] = hbuf[0] + hbuf[1]
+    head_step(2, 4, "x", x, 17)
+
+    groups(2, 6)
+
+    for axis, mine, buf, got, aug, sem in stages:
         right, to_right = along(axis, 1)
         left, to_left = along(axis, 3)
         wait_recv(aug, sem + 9)
@@ -384,25 +398,12 @@
         rcopy(buf.at[to_right, near], got.at[0, near], sem, right).start()
         rcopy(buf.at[to_left, far], got.at[1, far], sem, left).start()
 
-    @pl.loop(2, 4)
-    def _(j):
-        return_block(j)
-
-    recv_r[me] = send_r[me]
-
-    def head_step(base, count, axis, mine, sem):
-        for k in range(1, count):
-            dev, _ = along(axis, k)
-            rcopy(hbuf.at[base + mine], hbuf.at[base + mine], sem, dev).start()
-
-    wait_recv(hbuf.at[0], 13)
-    wait_send(hbuf.at[0], 13)
-    hbuf[2 + x] = hbuf[0] + hbuf[1]
-    head_step(2, 4, "x", x, 17)
-
-    def add3(own, got, out, sec):
-        total = own[sec].astype(F32) + got[0, sec].astype(F32) + got[1, sec].astype(F32)
-        out[sec] = total.astype(BF)
+    wait_recv(hbuf.at[pl.ds(2, 3)], 17)
+    wait_send(hbuf.at[pl.ds(2, 3)], 17)
+    hbuf[6 + y] = hbuf[2] + hbuf[3] + hbuf[4] + hbuf[5]
+    head_step(6, 4, "y", y, 20)
+
+    groups(6, 9)
 
     node_out[...] = jnp.zeros_like(node_out)
 
@@ -414,6 +415,10 @@
             cols = slice(n * 256, (n + 1) * 256)
             node_out[:, cols] = node_out[:, cols] + dot(hot_t[b], collect((0, 1, 2, 3), n))
 
+    def add3(own, got, out, sec):
+        total = own[sec].astype(F32) + got[0, sec].astype(F32) + got[1, sec].astype(F32)
+        out[sec] = total.astype(BF)
+
     wait_recv(ra, 15)
 
     @pl.loop(0, 4)
@@ -433,14 +438,12 @@
         dev, at_x = along("x", k)
         rcopy(sb.at[at_x], r2b.at[k - 1], 19, dev).start()
 
-    @pl.loop(0, 1)
-    def _(j):
-        land_block(j)
-
-    wait_recv(hbuf.at[pl.ds(2, 3)], 17)
-    wait_send(hbuf.at[pl.ds(2, 3)], 17)
-    hbuf[6 + y] = hbuf[2] + hbuf[3] + hbuf[4] + hbuf[5]
-    head_step(6, 4, "y", y, 20)
+    groups(9, 12)
+
+    wait_recv(hbuf.at[pl.ds(6, 3)], 20)
+    wait_send(hbuf.at[pl.ds(6, 3)], 20)
+    hbuf[10 + z] = hbuf[6] + hbuf[7] + hbuf[8] + hbuf[9]
+    head_step(10, 8, "z", z, 23)
 
     wait_recv(r2a, 18)
     total = sa[y].astype(F32) + r2a[0].astype(F32) + r2a[1].astype(F32) + r2a[2].astype(F32)
@@ -455,12 +458,10 @@
         dev, at_z = along("z", k)
         rcopy(tb.at[at_z], r3b.at[k - 1], 22, dev).start()
 
-    wait_recv(hbuf.at[pl.ds(6, 3)], 20)
-    wait_send(hbuf.at[pl.ds(6, 3)], 20)
-    hbuf[10 + z] = hbuf[6] + hbuf[7] + hbuf[8] + hbuf[9]
-    head_step(10, 8, "z", z, 23)
-
-    @pl.loop(1, 3)
+    groups(12, 16)
+    recv_r[me] = send_r[me]
+
+    @pl.loop(0, 3)
     def _(j):
         land_block(j)
 

time: 140 us -> 146 us (1.043)
  the two profiles are of different devices: /device:TPU:1 before, /device:TPU:25 now
where the time goes in v3:
time: 146 us; the launch traced here: 145 us
  Pallas kernels  145 us (99%)
    pallas_call x1, Pallas kernels, shards(): pl.pallas_call(body, out_shape=(jax.ShapeDtypeStruct((ROWS, WIDTH), F32),...  142 us

profile of v3, /device:TPU:25, one launch (start us, length us, event | category | flops | bytes accessed | tf_op | source)
XLA Modules:
  0.0 145.5 jit_solution(2601179435182801211)
XLA Ops:
  0.6 142.0 %shard_map.110 = (f32[384,1024]{1,0:T(8,128)}, f32[16,1024]{1,0:T(8,128)}) custom-call(s32[2,128]{1,0:T(2,128)} %bitcast.4, f32[1,128]{1,0:T(1,128)} %bitcast.5, bf16[1024]{0:T(1024)(128)(2,1)} %sw_in.1, s32[768,128]{1,0:T(8,128)} %bitcast.3, bf16[384,1024]{1,0:T(8,128)(2,1)} %emb_hbm.1, bf16[2048,1024]{1,0:T(8,128)(2,1)} %w1_hbm.1, bf16[1024,1024]{1,0:T(8,128)(2,1)} %w2_hbm.1), custom_call_target="tpu_custom_call" | custom-call | tf_op jit(solution)/shard_map/pallas_call | solution.py:558
  142.7 2.8 %shard_map.111 = (f32[128]{0:T(128)}, f32[384,1024]{1,0:T(8,128)}, f32[8,1024]{1,0:T(8,128)}, f32[4,1024]{1,0:T(4,128)}, f32[1024]{0:T(1024)}) custom-call(f32[384,1024]{1,0:T(8,128)} %get-tuple-element.7.node_in, f32[16,1024]{1,0:T(8,128)} %get-tuple-element.8.small_in), custom_call_target="tpu_custom_call" | custom-call | tf_op jit(solution)/shard_map/pallas_call | solution.py:574

commit v4 on v3

--- a/solution.py
+++ b/solution.py
@@ -309,7 +309,7 @@
                 return_pack(i // 4)
             send_block(send_r, recv_r, i // 4, R, i % 4 * 2, i % 4 * 2 + 2)
 
-    groups(0, 2)
+    groups(0, 4)
 
     for i in range(4):
         cols = slice(i * 256, (i + 1) * 256)
@@ -383,7 +383,7 @@
     hbuf[2 + x] = hbuf[0] + hbuf[1]
     head_step(2, 4, "x", x, 17)
 
-    groups(2, 6)
+    groups(4, 8)
 
     for axis, mine, buf, got, aug, sem in stages:
         right, to_right = along(axis, 1)
@@ -403,7 +403,7 @@
     hbuf[6 + y] = hbuf[2] + hbuf[3] + hbuf[4] + hbuf[5]
     head_step(6, 4, "y", y, 20)
 
-    groups(6, 9)
+    groups(8, 12)
 
     node_out[...] = jnp.zeros_like(node_out)
 
@@ -438,12 +438,17 @@
         dev, at_x = along("x", k)
         rcopy(sb.at[at_x], r2b.at[k - 1], 19, dev).start()
 
-    groups(9, 12)
+    groups(12, 16)
+    recv_r[me] = send_r[me]
 
     wait_recv(hbuf.at[pl.ds(6, 3)], 20)
     wait_send(hbuf.at[pl.ds(6, 3)], 20)
     hbuf[10 + z] = hbuf[6] + hbuf[7] + hbuf[8] + hbuf[9]
     head_step(10, 8, "z", z, 23)
+
+    @pl.loop(0, 1)
+    def _(j):
+        land_block(j)
 
     wait_recv(r2a, 18)
     total = sa[y].astype(F32) + r2a[0].astype(F32) + r2a[1].astype(F32) + r2a[2].astype(F32)
@@ -458,10 +463,7 @@
         dev, at_z = along("z", k)
         rcopy(tb.at[at_z], r3b.at[k - 1], 22, dev).start()
 
-    groups(12, 16)
-    recv_r[me] = send_r[me]
-
-    @pl.loop(0, 3)
+    @pl.loop(1, 3)
     def _(j):
         land_block(j)
 

time: 146 us -> 141 us (0.966)
  the two profiles are of different devices: /device:TPU:25 before, /device:TPU:1 now
where the time goes in v4:
time: 141 us
  Pallas kernels  140 us (99%)
    pallas_call x1, Pallas kernels, shards(): pl.pallas_call(body, out_shape=(jax.ShapeDtypeStruct((ROWS, WIDTH), F32),...  138 us
    pallas_call x1, Pallas kernels, shards(): pl.pallas_call(deliver, out_shape=(jax.ShapeDtypeStruct((EDGES,), F32), j...  2.83 us

profile of v4, /device:TPU:1, one launch (start us, length us, event | category | flops | bytes accessed | tf_op | source)
XLA Modules:
  0.0 141.1 jit_solution(5553266034843861459)
XLA Ops:
  0.6 137.6 %shard_map.110 = (f32[384,1024]{1,0:T(8,128)}, f32[16,1024]{1,0:T(8,128)}) custom-call(s32[2,128]{1,0:T(2,128)} %bitcast.4, f32[1,128]{1,0:T(1,128)} %bitcast.5, bf16[1024]{0:T(1024)(128)(2,1)} %sw_in.1, s32[768,128]{1,0:T(8,128)} %bitcast.3, bf16[384,1024]{1,0:T(8,128)(2,1)} %emb_hbm.1, bf16[2048,1024]{1,0:T(8,128)(2,1)} %w1_hbm.1, bf16[1024,1024]{1,0:T(8,128)(2,1)} %w2_hbm.1), custom_call_target="tpu_custom_call" | custom-call | tf_op jit(solution)/shard_map/pallas_call | solution.py:560
  138.2 2.8 %shard_map.111 = (f32[128]{0:T(128)}, f32[384,1024]{1,0:T(8,128)}, f32[8,1024]{1,0:T(8,128)}, f32[4,1024]{1,0:T(4,128)}, f32[1024]{0:T(1024)}) custom-call(f32[384,1024]{1,0:T(8,128)} %get-tuple-element.7.node_in, f32[16,1024]{1,0:T(8,128)} %get-tuple-element.8.small_in), custom_call_target="tpu_custom_call" | custom-call | tf_op jit(solution)/shard_map/pallas_call | solution.py:576

commit v5 on v4

--- a/solution.py
+++ b/solution.py
@@ -171,24 +171,26 @@
             out.append(jnp.concatenate([stage[0, rows, :], stage[1, rows, :]], axis=1))
         return jnp.concatenate(out, axis=0).astype(BF)
 
-    def send_block(src, dst, j, sem, first=0, last=8):
-        yy = (y + j) % 4
-
+    def send_pair(src, dst, p, sem, first=0, last=8):
         @pl.loop(first, last)
         def _(k):
             xx = (x + k % 4) % 4
             cc = (c + k // 4) % 2
-
-            def push(zz):
-                to = (yy * 4 + xx) * 16 + zz * 2 + cc
-                rcopy(src.at[to], dst.at[me], sem + j, ident(yy, zz, cc, xx)).start()
-
-            @pl.when(j + k > 0)
-            def _():
-                push(z)
-
-            for i in range(1, 8):
-                push((z + i) % 8)
+            for j in (p, p + 2):
+                yy = (y + j) % 4
+
+                def push(zz):
+                    to = (yy * 4 + xx) * 16 + zz * 2 + cc
+                    rcopy(src.at[to], dst.at[me], sem + j, ident(yy, zz, cc, xx)).start()
+
+                if j == 0:
+                    @pl.when(k > 0)
+                    def _():
+                        push(z)
+                else:
+                    push(z)
+                for i in range(1, 8):
+                    push((z + i) % 8)
 
     def wait_block(dst, j, sem):
         @pl.when(j == 0)
@@ -207,15 +209,17 @@
     G, R = 2, 6
     loads[1].wait()
 
-    @pl.loop(0, 4)
-    def _(j):
-        b = (y + j) % 4
-        for n in range(4):
-            part = dot(hot[b], emb[:, n * 256:(n + 1) * 256])
-            for s in range(4):
-                spread(s, n, part[s * 64:(s + 1) * 64])
-        pack(send_g, b)
-        send_block(send_g, recv_g, j, G)
+    for p in range(2):
+        @pl.loop(0, 2)
+        def _(i):
+            b = (y + p + 2 * i) % 4
+            for n in range(4):
+                part = dot(hot[b], emb[:, n * 256:(n + 1) * 256])
+                for s in range(4):
+                    spread(s, n, part[s * 64:(s + 1) * 64])
+            pack(send_g, b)
+
+        send_pair(send_g, recv_g, p, G)
 
     recv_g[me] = send_g[me]
 
@@ -251,7 +255,8 @@
             w2t[n * 256:(n + 1) * 256, rows] = w2[rows, n * 256:(n + 1) * 256].T
 
     @pl.loop(0, 4)
-    def _(j):
+    def _(i):
+        j = i % 2 * 2 + i // 2
         b = (y + 4 - j) % 4
         wait_block(recv_g, j, G)
         unpack(recv_g, b)
@@ -303,13 +308,13 @@
                     spread(side * 2 + k, n, part[k * 64:(k + 1) * 64])
         pack(send_r, b)
 
-    def groups(first, last):
-        for i in range(first, last):
-            if i % 4 == 0:
-                return_pack(i // 4)
-            send_block(send_r, recv_r, i // 4, R, i % 4 * 2, i % 4 * 2 + 2)
-
-    groups(0, 4)
+    def return_pair(p):
+        @pl.loop(0, 2)
+        def _(i):
+            return_pack(p + 2 * i)
+
+    return_pair(0)
+    send_pair(send_r, recv_r, 0, R, 0, 4)
 
     for i in range(4):
         cols = slice(i * 256, (i + 1) * 256)
@@ -383,7 +388,8 @@
     hbuf[2 + x] = hbuf[0] + hbuf[1]
     head_step(2, 4, "x", x, 17)
 
-    groups(4, 8)
+    send_pair(send_r, recv_r, 0, R, 4, 8)
+    return_pair(1)
 
     for axis, mine, buf, got, aug, sem in stages:
         right, to_right = along(axis, 1)
@@ -403,7 +409,7 @@
     hbuf[6 + y] = hbuf[2] + hbuf[3] + hbuf[4] + hbuf[5]
     head_step(6, 4, "y", y, 20)
 
-    groups(8, 12)
+    send_pair(send_r, recv_r, 1, R, 0, 4)
 
     node_out[...] = jnp.zeros_like(node_out)
 
@@ -438,7 +444,7 @@
         dev, at_x = along("x", k)
         rcopy(sb.at[at_x], r2b.at[k - 1], 19, dev).start()
 
-    groups(12, 16)
+    send_pair(send_r, recv_r, 1, R, 4, 8)
     recv_r[me] = send_r[me]
 
     wait_recv(hbuf.at[pl.ds(6, 3)], 20)
@@ -463,7 +469,7 @@
         dev, at_z = along("z", k)
         rcopy(tb.at[at_z], r3b.at[k - 1], 22, dev).start()
 
-    @pl.loop(1, 3)
+    @pl.loop(2, 3)
     def _(j):
         land_block(j)
 
@@ -488,9 +494,9 @@
         head += hbuf[10 + k]
     small_out[12:13, :] = head
 
-    @pl.loop(3, 4)
-    def _(j):
-        land_block(j)
+    @pl.loop(0, 2)
+    def _(i):
+        land_block(1 + 2 * i)
 
     wait_send(fifteen, 0)
     wait_send(idx.at[pl.ds(0, 240)], 1)

time: 141 us -> 137 us (0.972)
  Pallas kernels: 140 us -> 136 us
    pallas_call x1, Pallas kernels: 138 us -> 134 us  [shards(): pl.pallas_call(body, out_shape=(jax.ShapeDtypeStruct((ROWS, WIDTH), F32),...]
where the time goes in v5:
time: 137 us
  Pallas kernels  136 us (99%)
    pallas_call x1, Pallas kernels, shards(): pl.pallas_call(body, out_shape=(jax.ShapeDtypeStruct((ROWS, WIDTH), F32),...  134 us
    pallas_call x1, Pallas kernels, shards(): pl.pallas_call(deliver, out_shape=(jax.ShapeDtypeStruct((EDGES,), F32), j...  2.83 us

profile of v5, /device:TPU:1, one launch (start us, length us, event | category | flops | bytes accessed | tf_op | source)
XLA Modules:
  0.0 137.1 jit_solution(3656108380997808281)
XLA Ops:
  0.6 133.6 %shard_map.110 = (f32[384,1024]{1,0:T(8,128)}, f32[16,1024]{1,0:T(8,128)}) custom-call(s32[2,128]{1,0:T(2,128)} %bitcast.4, f32[1,128]{1,0:T(1,128)} %bitcast.5, bf16[1024]{0:T(1024)(128)(2,1)} %sw_in.1, s32[768,128]{1,0:T(8,128)} %bitcast.3, bf16[384,1024]{1,0:T(8,128)(2,1)} %emb_hbm.1, bf16[2048,1024]{1,0:T(8,128)(2,1)} %w1_hbm.1, bf16[1024,1024]{1,0:T(8,128)(2,1)} %w2_hbm.1), custom_call_target="tpu_custom_call" | custom-call | tf_op jit(solution)/shard_map/pallas_call | solution.py:566
  134.3 2.8 %shard_map.111 = (f32[128]{0:T(128)}, f32[384,1024]{1,0:T(8,128)}, f32[8,1024]{1,0:T(8,128)}, f32[4,1024]{1,0:T(4,128)}, f32[1024]{0:T(1024)}) custom-call(f32[384,1024]{1,0:T(8,128)} %get-tuple-element.7.node_in, f32[16,1024]{1,0:T(8,128)} %get-tuple-element.8.small_in), custom_call_target="tpu_custom_call" | custom-call | tf_op jit(solution)/shard_map/pallas_call | solution.py:582

commit v6 on v5

--- a/solution.py
+++ b/solution.py
@@ -46,7 +46,7 @@
     table, emb, w1, w2, w1t, w2t, idx, hot, hot_t, picks, picks_t, stage,
     send_g, recv_g, send_r, recv_r,
     feats, first_act, first_slope, ft_own, ft, at_own, at, d1, d2, fg,
-    pa, pb, ra, rb, ua, ub, sa, sb, r2a, r2b, ta, tb, r3a, r3b, hbuf,
+    pa, pb, ra, rb, ua, ub, sa, sb, r2a, r2b, ta, tb, r3a, r3b, hbuf, node, second_act,
     fifteen, load_sem, ss, rs,
 ):
     dom = lax.axis_index("dom")
@@ -174,10 +174,10 @@
     def send_pair(src, dst, p, sem, first=0, last=8):
         @pl.loop(first, last)
         def _(k):
-            xx = (x + k % 4) % 4
             cc = (c + k // 4) % 2
             for j in (p, p + 2):
                 yy = (y + j) % 4
+                xx = (x + (k + j - p) % 4) % 4
 
                 def push(zz):
                     to = (yy * 4 + xx) * 16 + zz * 2 + cc
@@ -274,19 +274,15 @@
         first_act[:, cols] = act
         first_slope[:, cols] = slope
 
-    score = jnp.zeros((1, 128), F32)
     sgrad = jnp.sum(jnp.where(eye, sgrad_in[...], 0.0), axis=1, keepdims=True)
     for n in range(4):
         cols = slice(n * 256, (n + 1) * 256)
         act, slope = gelu_both(dot(first_act[...], w2[:, cols]))
         act = act.astype(BF)
         sw = sw_in[cols].reshape(1, 256)
-        score += dot_nt(jnp.broadcast_to(sw, (8, 256)), act)[0:1]
-        hbuf[0, :, cols] = jnp.sum(sgrad * act.astype(F32), axis=0, keepdims=True)
+        second_act[:, cols] = act
         d2[0:128, cols] = (sgrad * sw.astype(F32) * slope).astype(BF)
-    small_out[13:14, 0:128] = score
     rcopy(d2.at[pl.ds(0, 128)], d2.at[pl.ds(128, 128)], 12, other).start()
-    rcopy(hbuf.at[0], hbuf.at[1], 13, other).start()
 
     for n in range(4):
         cols = slice(n * 256, (n + 1) * 256)
@@ -315,6 +311,15 @@
 
     return_pair(0)
     send_pair(send_r, recv_r, 0, R, 0, 4)
+
+    score = jnp.zeros((1, 128), F32)
+    for n in range(4):
+        cols = slice(n * 256, (n + 1) * 256)
+        act = second_act[:, cols]
+        hbuf[0, :, cols] = jnp.sum(sgrad * act.astype(F32), axis=0, keepdims=True)
+        score += dot_nt(jnp.broadcast_to(sw_in[cols].reshape(1, 256), (8, 256)), act)[0:1]
+    small_out[13:14, 0:128] = score
+    rcopy(hbuf.at[0], hbuf.at[1], 13, other).start()
 
     for i in range(4):
         cols = slice(i * 256, (i + 1) * 256)
@@ -411,7 +416,7 @@
 
     send_pair(send_r, recv_r, 1, R, 0, 4)
 
-    node_out[...] = jnp.zeros_like(node_out)
+    node[...] = jnp.zeros_like(node)
 
     def land_block(j):
         b = (y + 4 - j) % 4
@@ -419,7 +424,7 @@
         unpack(recv_r, b)
         for n in range(4):
             cols = slice(n * 256, (n + 1) * 256)
-            node_out[:, cols] = node_out[:, cols] + dot(hot_t[b], collect((0, 1, 2, 3), n))
+            node[:, cols] = node[:, cols] + dot(hot_t[b], collect((0, 1, 2, 3), n))
 
     def add3(own, got, out, sec):
         total = own[sec].astype(F32) + got[0, sec].astype(F32) + got[1, sec].astype(F32)
@@ -494,9 +499,16 @@
         head += hbuf[10 + k]
     small_out[12:13, :] = head
 
-    @pl.loop(0, 2)
-    def _(i):
-        land_block(1 + 2 * i)
+    land_block(1)
+    b = (y + 1) % 4
+    wait_block(recv_r, 3, R)
+    unpack(recv_r, b)
+    outs = []
+    for n in range(4):
+        cols = slice(n * 256, (n + 1) * 256)
+        node[:, cols] = node[:, cols] + dot(hot_t[b], collect((0, 1, 2, 3), n))
+        outs.append(pltpu.make_async_copy(node.at[:, cols], node_out.at[:, cols], load_sem.at[n]))
+        outs[n].start()
 
     wait_send(fifteen, 0)
     wait_send(idx.at[pl.ds(0, 240)], 1)
@@ -515,6 +527,8 @@
     wait_send(r3a, 21)
     wait_send(r3b, 22)
     wait_send(hbuf.at[pl.ds(10, 7)], 23)
+    for out in outs:
+        out.wait()
 
 
 def deliver(node_in, small_in, score_out, node_out, first_out, second_out, head_out, held, small, sem_in, sem_out):
@@ -559,7 +573,7 @@
         V((3, 8, 16, 384), BF), V((3, 8, 16, 384), BF),
         V((8, 16, 384), BF), V((8, 16, 384), BF),
         V((7, 16, 384), BF), V((7, 16, 384), BF),
-        V((18, 1, HID), F32),
+        V((18, 1, HID), F32), V((ROWS, WIDTH), F32), V((EDGES, HID), BF),
         V((15, 1, 2 * EDGES), jnp.int32),
         pltpu.SemaphoreType.DMA((4,)), pltpu.SemaphoreType.DMA((26,)), pltpu.SemaphoreType.DMA((26,)),
     ]
@@ -570,7 +584,7 @@
             jax.ShapeDtypeStruct((16, HID), F32),
         ),
         in_specs=[vm] * 3 + [hbm] * 4,
-        out_specs=(vm, vm),
+        out_specs=(hbm, vm),
         scratch_shapes=scratch,
         compiler_params=pltpu.CompilerParams(
             collective_id=0, has_side_effects=True, vmem_limit_bytes=58 * 2**20

time: 137 us -> 137 us (level); the launches traced: 137 us -> 135 us
    pallas_call x1, Pallas kernels: 134 us -> 132 us  [shards(): pl.pallas_call(body, out_shape=(jax.ShapeDtypeStruct((ROWS, WIDTH), F32),...]
where the time goes in v6:
time: 137 us; the launch traced here: 135 us
  Pallas kernels  135 us (99%)
    pallas_call x1, Pallas kernels, shards(): pl.pallas_call(body, out_shape=(jax.ShapeDtypeStruct((ROWS, WIDTH), F32),...  132 us
    pallas_call x1, Pallas kernels, shards(): pl.pallas_call(deliver, out_shape=(jax.ShapeDtypeStruct((EDGES,), F32), j...  2.83 us

profile of v6, /device:TPU:1, one launch (start us, length us, event | category | flops | bytes accessed | tf_op | source)
XLA Modules:
  0.0 135.5 jit_solution(13230754606502892445)
XLA Ops:
  0.6 132.0 %shard_map.110 = (f32[384,1024]{1,0:T(8,128)}, f32[16,1024]{1,0:T(8,128)}) custom-call(s32[2,128]{1,0:T(2,128)} %bitcast.4, f32[1,128]{1,0:T(1,128)} %bitcast.5, bf16[1024]{0:T(1024)(128)(2,1)} %sw_in.1, s32[768,128]{1,0:T(8,128)} %bitcast.3, bf16[384,1024]{1,0:T(8,128)(2,1)} %emb_hbm.1, bf16[2048,1024]{1,0:T(8,128)(2,1)} %w1_hbm.1, bf16[1024,1024]{1,0:T(8,128)(2,1)} %w2_hbm.1), custom_call_target="tpu_custom_call" | custom-call | tf_op jit(solution)/shard_map/pallas_call | solution.py:580
  132.6 2.8 %shard_map.111 = (f32[128]{0:T(128)}, f32[384,1024]{1,0:T(8,128)}, f32[8,1024]{1,0:T(8,128)}, f32[4,1024]{1,0:T(4,128)}, f32[1024]{0:T(1024)}) custom-call(f32[384,1024]{1,0:T(8,128)} %get-tuple-element.7.node_in, f32[16,1024]{1,0:T(8,128)} %get-tuple-element.8.small_in), custom_call_target="tpu_custom_call" | custom-call | tf_op jit(solution)/shard_map/pallas_call | solution.py:596

commit v7 on v6

--- a/solution.py
+++ b/solution.py
@@ -46,7 +46,7 @@
     table, emb, w1, w2, w1t, w2t, idx, hot, hot_t, picks, picks_t, stage,
     send_g, recv_g, send_r, recv_r,
     feats, first_act, first_slope, ft_own, ft, at_own, at, d1, d2, fg,
-    pa, pb, ra, rb, ua, ub, sa, sb, r2a, r2b, ta, tb, r3a, r3b, hbuf, node, second_act,
+    pa, pb, ra, rb, sa, sb, r2a, r2b, ta, tb, r3a, r3b, hbuf, node, second_act,
     fifteen, load_sem, ss, rs,
 ):
     dom = lax.axis_index("dom")
@@ -372,16 +372,11 @@
             return ident((y + k) % 4, z, c, x), (y + k) % 4
         return ident(y, (z + k) % 8, c, x), (z + k) % 8
 
-    near, far = pl.ds(0, 2), pl.ds(2, 2)
-    stages = (("x", x, pa, ra, ua, 15), ("y", y, pb, rb, ub, 16))
-    for axis, mine, buf, got, aug, sem in stages:
-        right, to_right = along(axis, 1)
-        left, to_left = along(axis, 3)
-        opposite = (mine + 2) % 4
-        rcopy(buf.at[opposite, near], aug.at[0], sem + 9, right).start()
-        rcopy(buf.at[opposite, far], aug.at[1], sem + 9, left).start()
-        rcopy(buf.at[to_right, far], got.at[0, far], sem, right).start()
-        rcopy(buf.at[to_left, near], got.at[1, near], sem, left).start()
+    for k in range(1, 4):
+        dev, at_x = along("x", k)
+        rcopy(pa.at[at_x], ra.at[k - 1], 15, dev).start()
+        dev, at_y = along("y", k)
+        rcopy(pb.at[at_y], rb.at[k - 1], 16, dev).start()
 
     def head_step(base, count, axis, mine, sem):
         for k in range(1, count):
@@ -396,18 +391,6 @@
     send_pair(send_r, recv_r, 0, R, 4, 8)
     return_pair(1)
 
-    for axis, mine, buf, got, aug, sem in stages:
-        right, to_right = along(axis, 1)
-        left, to_left = along(axis, 3)
-        wait_recv(aug, sem + 9)
-
-        @pl.loop(0, 2)
-        def _(i):
-            buf[to_right, i] = (buf[to_right, i].astype(F32) + aug[0, i].astype(F32)).astype(BF)
-            buf[to_left, 2 + i] = (buf[to_left, 2 + i].astype(F32) + aug[1, i].astype(F32)).astype(BF)
-
-        rcopy(buf.at[to_right, near], got.at[0, near], sem, right).start()
-        rcopy(buf.at[to_left, far], got.at[1, far], sem, left).start()
 
     wait_recv(hbuf.at[pl.ds(2, 3)], 17)
     wait_send(hbuf.at[pl.ds(2, 3)], 17)
@@ -426,15 +409,15 @@
             cols = slice(n * 256, (n + 1) * 256)
             node[:, cols] = node[:, cols] + dot(hot_t[b], collect((0, 1, 2, 3), n))
 
-    def add3(own, got, out, sec):
-        total = own[sec].astype(F32) + got[0, sec].astype(F32) + got[1, sec].astype(F32)
+    def add4(own, got, out, sec):
+        total = own[sec].astype(F32) + got[0, sec].astype(F32) + got[1, sec].astype(F32) + got[2, sec].astype(F32)
         out[sec] = total.astype(BF)
 
     wait_recv(ra, 15)
 
     @pl.loop(0, 4)
     def _(i):
-        add3(pa.at[x], ra, sa, i)
+        add4(pa.at[x], ra, sa, i)
 
     for k in range(1, 4):
         dev, at_y = along("y", k)
@@ -443,7 +426,7 @@
 
     @pl.loop(0, 4)
     def _(i):
-        add3(pb.at[y], rb, sb, i)
+        add4(pb.at[y], rb, sb, i)
 
     for k in range(1, 4):
         dev, at_x = along("x", k)
@@ -520,8 +503,6 @@
     wait_send(d1.at[pl.ds(0, 128)], 14)
     wait_send(ra, 15)
     wait_send(rb, 16)
-    wait_send(ua, 24)
-    wait_send(ub, 25)
     wait_send(r2a, 18)
     wait_send(r2b, 19)
     wait_send(r3a, 21)
@@ -567,15 +548,14 @@
         V((32, 2, 16, EDGES), BF), V((32, 16, 2 * EDGES), BF),
         V((2 * EDGES, HID), BF), V((2 * EDGES, HID), BF), V((EDGES, 2 * WIDTH), BF),
         V((4, 4, 8, 16, 384), BF), V((4, 4, 8, 16, 384), BF),
-        V((2, 4, 8, 16, 384), BF), V((2, 4, 8, 16, 384), BF),
-        V((2, 2, 8, 16, 384), BF), V((2, 2, 8, 16, 384), BF),
+        V((3, 4, 8, 16, 384), BF), V((3, 4, 8, 16, 384), BF),
         V((4, 8, 16, 384), BF), V((4, 8, 16, 384), BF),
         V((3, 8, 16, 384), BF), V((3, 8, 16, 384), BF),
         V((8, 16, 384), BF), V((8, 16, 384), BF),
         V((7, 16, 384), BF), V((7, 16, 384), BF),
         V((18, 1, HID), F32), V((ROWS, WIDTH), F32), V((EDGES, HID), BF),
         V((15, 1, 2 * EDGES), jnp.int32),
-        pltpu.SemaphoreType.DMA((4,)), pltpu.SemaphoreType.DMA((26,)), pltpu.SemaphoreType.DMA((26,)),
+        pltpu.SemaphoreType.DMA((4,)), pltpu.SemaphoreType.DMA((24,)), pltpu.SemaphoreType.DMA((24,)),
     ]
     node, small = pl.pallas_call(
         body,

time: 137 us -> 145 us (1.058)
  Pallas kernels: 135 us -> 143 us
    pallas_call x1, Pallas kernels: 132 us -> 140 us  [shards(): pl.pallas_call(body, out_shape=(jax.ShapeDtypeStruct((ROWS, WIDTH), F32),...]
where the time goes in v7:
time: 145 us; the launch traced here: 144 us
  Pallas kernels  143 us (99%)
    pallas_call x1, Pallas kernels, shards(): pl.pallas_call(body, out_shape=(jax.ShapeDtypeStruct((ROWS, WIDTH), F32),...  140 us

profile of v7, /device:TPU:1, one launch (start us, length us, event | category | flops | bytes accessed | tf_op | source)
XLA Modules:
  0.0 143.8 jit_solution(11190022195726528400)
XLA Ops:
  0.6 140.4 %shard_map.110 = (f32[384,1024]{1,0:T(8,128)}, f32[16,1024]{1,0:T(8,128)}) custom-call(s32[2,128]{1,0:T(2,128)} %bitcast.4, f32[1,128]{1,0:T(1,128)} %bitcast.5, bf16[1024]{0:T(1024)(128)(2,1)} %sw_in.1, s32[768,128]{1,0:T(8,128)} %bitcast.3, bf16[384,1024]{1,0:T(8,128)(2,1)} %emb_hbm.1, bf16[2048,1024]{1,0:T(8,128)(2,1)} %w1_hbm.1, bf16[1024,1024]{1,0:T(8,128)(2,1)} %w2_hbm.1), custom_call_target="tpu_custom_call" | custom-call | tf_op jit(solution)/shard_map/pallas_call | solution.py:560
  141.0 2.8 %shard_map.111 = (f32[128]{0:T(128)}, f32[384,1024]{1,0:T(8,128)}, f32[8,1024]{1,0:T(8,128)}, f32[4,1024]{1,0:T(4,128)}, f32[1024]{0:T(1024)}) custom-call(f32[384,1024]{1,0:T(8,128)} %get-tuple-element.7.node_in, f32[16,1024]{1,0:T(8,128)} %get-tuple-element.8.small_in), custom_call_target="tpu_custom_call" | custom-call | tf_op jit(solution)/shard_map/pallas_call | solution.py:576
